TPU v7x, 32 devices: a whole 2x2x4 slice. The times are simulated.
32 devices in a mesh: blk: 8 (over z, x), blade: 4 (over y, core).
Axes of the slice: x: 2, y: 2, z: 4, core: 2. Of those that a mesh axis runs over, the one named last changes fastest.
Arguments:
- bnd_pos: float32 [3, 2048], P(None, 'blk'), may hold values from -1 to 1
- bnd_owner: int32 [2048, 1], P('blk'), may hold values from 0 to 7; in each aligned block of 256 rows (0 to 255, 256 to 511, ...) at most 64 rows name the same one
- bnd_slot: int32 [2048], P('blk'), may hold values from 0 to 16383
- seg_start: float32 [3, 4, 1024], P(None, 'blade', 'blk'), may hold values from -1 to 1
- seg_step: float32 [3, 4, 1024], P(None, 'blade', 'blk'), may hold values from -0.15 to 0.15
- seg_gamma: float32 [4, 1024], P('blade', 'blk'), may hold values from -6 to 6
- seg_sec: int32 [4, 1024], P('blade', 'blk'), may hold values from 0 to 63
- flow: float32 [3, 64, 64, 256], P(None, 'blk', 'blade'), may hold values from -6 to 6
- source: float32 [3, 64, 64, 256], P(None, 'blk', 'blade'), may hold values from -6 to 6
- extra_diag: float32 [64, 64, 256], P('blk', 'blade'), may hold values from 0.25 to 2
- circ_weight: float32 [64, 64, 256], P('blk', 'blade'), may hold values from -0.125 to 0.125
- sec_block: int32 [4, 64], replicated, may hold values from 0 to 7
- sec_row: int32 [4, 64], replicated, may hold values from 0 to 15
Outputs:
- new_flow: float32 [3, 64, 64, 256], P(None, 'blk', 'blade')
- new_gamma: float32 [4, 1024], P('blade', 'blk')
Inputs may be any that keep to these rules, and one draw needn't show every extreme that they name: `bnd_owner`: among the 256 boundary cells of each aligned block (one index of blk), at most 64 have the same owner, and some owner has exactly 64.
All inputs are finite; a program needn't handle non-finite values.
Results may differ from a plain program's by a relative error of at most 0.0001.
Values sent between devices are 32-bit elements; how exact they have to be, the bound alone decides.
A program may use at most 64 MiB of HBM per device.

v0:
```python
import functools
import math

import jax
import jax.numpy as jnp
from jax import lax
from jax.experimental import pallas as pl
from jax.experimental.pallas import tpu as pltpu
from jax.sharding import PartitionSpec as P

CORE = 0.01
FOUR_PI = 4.0 * math.pi
OMEGA = 0.8
RELAX = 0.5
LANES = 128
MESH = pl.DeviceIdType.MESH


def kernel(
    n_blk,
    n_bld,
    pos_hbm,
    own_hbm,
    slot_hbm,
    start_hbm,
    step_hbm,
    gam_hbm,
    sec_hbm,
    sblk_hbm,
    srow_hbm,
    flow_ref,
    src_ref,
    diag_ref,
    circ_ref,
    out_ref,
    ng_hbm,
    pos_ref,
    own_ref,
    slot_ref,
    start_ref,
    step_ref,
    gam_ref,
    sec_ref,
    sblk_ref,
    srow_ref,
    ng_ref,
    gath,
    vel,
    prof,
    flow_v,
    mid_v,
    out_v,
    src_v,
    diag_v,
    circ_v,
    m_v,
    ysend,
    yrecv,
    dgn_v,
    pos8,
    post,
    pb,
    keys,
    zt,
    lhs,
    sem_in,
    sem_out,
    wake_send,
    wake_recv,
    vel_send,
    vel_recv,
    prof_send,
    prof_recv,
    halo_send,
    halo_recv,
):
    n = n_blk * n_bld
    b = lax.axis_index("blk")
    j = lax.axis_index("blade")
    me = b * n_bld + j
    _, cx, cy, cz = src_v.shape
    half = pb.shape[1]
    n_pair = n // 2
    zbits = cz.bit_length() - 1

    def dev(d):
        return (lax.div(d, n_bld), lax.rem(d, n_bld))

    small = [
        pltpu.make_async_copy(source, target, sem_in.at[4 + k])
        for k, (source, target) in enumerate(
            (
                (start_hbm, start_ref),
                (step_hbm, step_ref),
                (gam_hbm, gam_ref),
                (slot_hbm, slot_ref),
                (own_hbm, own_ref),
                (pos_hbm, pos_ref),
                (sec_hbm, sec_ref),
                (sblk_hbm, sblk_ref),
                (srow_hbm, srow_ref),
            )
        )
    ]
    for copy in small:
        copy.start()
    loads = [
        pltpu.make_async_copy(flow_ref, flow_v.at[:, pl.ds(1, cx)], sem_in.at[0]),
        pltpu.make_async_copy(diag_ref, diag_v, sem_in.at[1]),
        pltpu.make_async_copy(src_ref, src_v, sem_in.at[2]),
        pltpu.make_async_copy(circ_ref, circ_v, sem_in.at[3]),
    ]
    for copy in loads:
        copy.start()

    barrier = pltpu.get_barrier_semaphore()

    @pl.loop(1, n)
    def _(i):
        pl.semaphore_signal(
            barrier, inc=1, device_id=dev(lax.rem(me + i, n)), device_id_type=MESH
        )

    for copy in small:
        copy.wait()

    lane1 = lax.broadcasted_iota(jnp.int32, (8, LANES), 1)
    low1 = lane1 < half
    slot_row = jnp.broadcast_to(
        slot_ref[pl.ds(lax.div(j, 2), 1), :].astype(jnp.float32), (8, LANES)
    )
    own_row = jnp.broadcast_to(
        own_ref[pl.ds(lax.div(j, 2), 1), :].astype(jnp.float32), (8, LANES)
    )
    mine_low = lax.rem(j, 2) == 0
    own_row = pltpu.roll(own_row, half, 1)
    first = jnp.where(low1, slot_row, own_row)
    second = jnp.where(low1, own_row, slot_row)
    tag = jnp.where(mine_low, first, second)
    gath[me, 0:3, :] = start_ref[:, 0, :]
    gath[me, 3:6, :] = step_ref[:, 0, :]
    gath[me, 6:7, :] = gam_ref[...]
    gath[me, 7:8, :] = tag[0:1, :]

    pl.semaphore_wait(barrier, n - 1)

    def wake_copy(dst, slot):
        return pltpu.make_async_remote_copy(
            src_ref=gath.at[me],
            dst_ref=gath.at[me],
            send_sem=wake_send.at[slot],
            recv_sem=wake_recv.at[me],
            device_id=dev(dst),
            device_id_type=MESH,
        )

    @pl.loop(1, n)
    def _(i):
        wake_copy(lax.rem(me + i, n), i).start()

    has = (b < n_blk - 1, b > 0, j < n_bld - 1, j > 0)
    nxt_b, prv_b = (b + 1, j), (b - 1, j)
    nxt_j, prv_j = (b, j + 1), (b, j - 1)

    def halo_copies(stage):
        base = 4 * stage
        to_next = flow_ref.at[:, cx - 1] if stage == 0 else mid_v.at[:, cx]
        to_prev = flow_ref.at[:, 0] if stage == 0 else mid_v.at[:, 1]
        grid = flow_v if stage == 0 else mid_v
        pairs = [
            (to_next, grid.at[:, 0], nxt_b, 0),
            (to_prev, grid.at[:, cx + 1], prv_b, 1),
            (ysend.at[stage, 0], yrecv.at[stage, 0], nxt_j, 2),
            (ysend.at[stage, 1], yrecv.at[stage, 1], prv_j, 3),
        ]
        return [
            pltpu.make_async_remote_copy(
                src_ref=s,
                dst_ref=d,
                send_sem=halo_send.at[base + k],
                recv_sem=halo_recv.at[base + k],
                device_id=to,
                device_id_type=MESH,
            )
            for s, d, to, k in pairs
        ]

    def guarded(cond, action):
        @pl.when(cond)
        def _():
            action()

    diag_copy = pltpu.make_async_remote_copy(
        src_ref=diag_ref.at[0],
        dst_ref=dgn_v,
        send_sem=halo_send.at[8],
        recv_sem=halo_recv.at[8],
        device_id=prv_b,
        device_id_type=MESH,
    )
    halo0 = halo_copies(0)
    halo1 = halo_copies(1)
    guarded(has[0], halo0[0].start)
    guarded(has[1], halo0[1].start)

    arrives = (has[1], has[0], has[3], has[2])

    @pl.when(b == 0)
    def _():
        flow_v[:, 0] = jnp.zeros((3, cy, cz), jnp.float32)
        mid_v[:, 0] = jnp.zeros((3, cy, cz), jnp.float32)

    @pl.when(b == n_blk - 1)
    def _():
        flow_v[:, cx + 1] = jnp.zeros((3, cy, cz), jnp.float32)
        mid_v[:, cx + 1] = jnp.zeros((3, cy, cz), jnp.float32)
        dgn_v[...] = jnp.zeros((cy, cz), jnp.float32)

    @pl.when(j == 0)
    def _():
        yrecv[:, 0] = jnp.zeros(yrecv.shape[:1] + yrecv.shape[2:], jnp.float32)

    @pl.when(j == n_bld - 1)
    def _():
        yrecv[:, 1] = jnp.zeros(yrecv.shape[:1] + yrecv.shape[2:], jnp.float32)

    loads[0].wait()
    loads[1].wait()
    for c in range(3):
        ysend[0, 0, c] = flow_v[c, 1 : cx + 1, cy - 1, :]
        ysend[0, 1, c] = flow_v[c, 1 : cx + 1, 0, :]
    ysend[0, 0, 3] = diag_v[:, cy - 1, :]
    ysend[0, 1, 3] = diag_v[:, 0, :]
    guarded(has[2], halo0[2].start)
    guarded(has[3], halo0[3].start)
    guarded(has[1], diag_copy.start)

    pos8[...] = jnp.zeros(pos8.shape, jnp.float32)
    pos8[0:3, :] = pos_ref[...]
    post[...] = pos8[...].T
    mine = post[pl.ds(pl.multiple_of(j * half, half), half), :]
    for c in range(3):
        pb[c] = jnp.broadcast_to(mine[:, c : c + 1], (half, LANES))

    n_sec = sblk_ref.shape[1]
    place = sblk_ref[pl.ds(j, 1), :] * cy + srow_ref[pl.ds(j, 1), :]
    place = jnp.broadcast_to(place.astype(jnp.float32), (n_sec, n_sec))
    eye = lax.broadcasted_iota(jnp.int32, (n_sec, n_sec), 0) == lax.broadcasted_iota(
        jnp.int32, (n_sec, n_sec), 1
    )
    place = jnp.sum(jnp.where(eye, place, 0.0), axis=1, keepdims=True)
    match = lax.broadcasted_iota(jnp.int32, (n_sec, LANES), 0) == sec_ref[...]
    seg_place = jnp.sum(jnp.where(match, place, 0.0), axis=0, keepdims=True)

    row_id = lax.broadcasted_iota(jnp.int32, (cy, cz), 0)
    col_id = lax.broadcasted_iota(jnp.int32, (cy, cz), 1)

    def beside_plane(u, left, right):
        total = jnp.where(row_id == 0, left, pltpu.roll(u, 1, 0))
        total += jnp.where(row_id == cy - 1, right, pltpu.roll(u, cy - 1, 0))
        total += jnp.where(col_id == 0, 0.0, pltpu.roll(u, 1, 1))
        total += jnp.where(col_id == cz - 1, 0.0, pltpu.roll(u, cz - 1, 1))
        return total

    def relaxed(grid, stage, c, x, m):
        u = grid[c, x + 1]
        left = yrecv[stage, 0, c, pl.ds(x, 1), :]
        right = yrecv[stage, 1, c, pl.ds(x, 1), :]
        beside = beside_plane(u, left, right) + grid[c, x] + grid[c, x + 2]
        return (1.0 - OMEGA) * u + m * (src_v[c, x] + beside)

    def induce(src, acc):
        rows = [jnp.broadcast_to(gath[src, r : r + 1, :], (8, LANES)) for r in range(7)]
        sx, sy, sz, dx, dy, dz, gam = rows
        dd = dx * dx + dy * dy + dz * dz
        bias = CORE * dd + CORE * CORE
        gam = gam * (1.0 / FOUR_PI)
        acc = list(acc)
        for g in range(half // 8):
            part = slice(8 * g, 8 * g + 8)
            rx, ry, rz = pb[0, part] - sx, pb[1, part] - sy, pb[2, part] - sz
            along_one = dx * rx + dy * ry + dz * rz
            along_two = along_one - dd
            sq_one = rx * rx + ry * ry + rz * rz + CORE
            sq_two = sq_one - along_one - along_two
            along = along_one * lax.rsqrt(sq_one) - along_two * lax.rsqrt(sq_two)
            kx = dy * rz - dz * ry
            ky = dz * rx - dx * rz
            kz = dx * ry - dy * rx
            w = gam * along / (kx * kx + ky * ky + kz * kz + bias)
            acc[3 * g] += w * kx
            acc[3 * g + 1] += w * ky
            acc[3 * g + 2] += w * kz
        return tuple(acc)

    zero = jnp.zeros((8, LANES), jnp.float32)
    acc = induce(me, (zero,) * (3 * (half // 8)))

    def wake_step(i, acc):
        src = lax.rem(me + n - i, n)
        pltpu.make_async_remote_copy(
            src_ref=gath.at[src],
            dst_ref=gath.at[src],
            send_sem=wake_send.at[i],
            recv_sem=wake_recv.at[src],
            device_id=dev(src),
            device_id_type=MESH,
        ).wait_recv()
        return induce(src, acc)

    middle = 5 * n // 8
    acc = lax.fori_loop(1, middle, wake_step, acc)

    loads[2].wait()
    for k in range(4):
        guarded(arrives[k], halo0[k].wait_recv)

    @pl.loop(0, cx)
    def _(x):
        m = OMEGA / (6.0 + diag_v[x])
        m_v[x] = m
        for c in range(3):
            mid_v[c, x + 1] = relaxed(flow_v, 0, c, x, m)

    for c in range(3):
        ysend[1, 0, c] = mid_v[c, 1 : cx + 1, cy - 1, :]
        ysend[1, 1, c] = mid_v[c, 1 : cx + 1, 0, :]
    ysend[1, 0, 3] = jnp.zeros((cx, cz), jnp.float32)
    ysend[1, 1, 3] = jnp.zeros((cx, cz), jnp.float32)
    for k in range(4):
        guarded(has[k], halo1[k].start)

    acc = lax.fori_loop(middle, n, wake_step, acc)
    ax, ay, az = (jnp.concatenate(acc[c::3], axis=0) for c in range(3))
    vel[me, 0:1, :] = jnp.sum(jnp.concatenate([ax, ay], axis=0).T, axis=0, keepdims=True)
    vel[me, 1:2, :] = jnp.sum(jnp.concatenate([az, az], axis=0).T, axis=0, keepdims=True)

    def vel_copy(dst, slot):
        return pltpu.make_async_remote_copy(
            src_ref=vel.at[me],
            dst_ref=vel.at[me],
            send_sem=vel_send.at[slot],
            recv_sem=vel_recv.at[0],
            device_id=dev(dst),
            device_id_type=MESH,
        )

    @pl.loop(1, n)
    def _(i):
        vel_copy(lax.rem(me + i, n), i).start()

    loads[3].wait()
    for k in range(4):
        guarded(arrives[k], halo1[k].wait_recv)

    def second(x, total):
        m = m_v[x]
        for c in range(3):
            u = relaxed(mid_v, 1, c, x, m)
            out_v[c, x] = u
            if c == 1:
                total += circ_v[x] * u
        return total

    profile = lax.fori_loop(0, cx, second, jnp.zeros((cy, cz), jnp.float32))
    store_inner = pltpu.make_async_copy(
        out_v.at[:, pl.ds(2, cx - 3)], out_ref.at[:, pl.ds(2, cx - 3)], sem_out.at[0]
    )
    store_inner.start()

    z_id = lax.broadcasted_iota(jnp.int32, (cz, LANES), 0)

    @pl.loop(0, n_pair, unroll=4)
    def _(q):
        even = jnp.broadcast_to(gath[2 * q, 7:8, :], (8, LANES))
        odd = jnp.broadcast_to(gath[2 * q + 1, 7:8, :], (8, LANES))
        slot = jnp.where(low1, even, odd).astype(jnp.int32)
        owner = pltpu.roll(jnp.where(low1, odd, even), half, 1).astype(jnp.int32)
        row = (slot >> zbits) - j * cy
        col = slot & (cz - 1)
        keys[q, 0] = jnp.where(owner == b, row, -4 * cy * n_bld)
        keys[q, 1] = jnp.where(owner == b + 1, row, -4 * cy * n_bld)
        cols = pl.ds(pl.multiple_of(q * LANES, LANES), LANES)
        zt[:, cols] = jnp.where(z_id == col[0:1, :], 1.0, 0.0).astype(jnp.bfloat16)

    y_id = lax.broadcasted_iota(jnp.int32, (cy, LANES), 0)
    edge_id = jnp.where(y_id >= 6, -2, jnp.where((y_id & 1) == 0, -1, cy))

    others = vel.at[pl.ds(0, n - 1)]
    pltpu.make_async_copy(others, others, vel_recv.at[0]).wait()

    n_row = 7 * cy

    @pl.loop(0, n_pair, unroll=4)
    def _(q):
        e0 = jnp.broadcast_to(vel[2 * q, 0:1, :], (8, LANES))
        e1 = jnp.broadcast_to(vel[2 * q, 1:2, :], (8, LANES))
        o0 = jnp.broadcast_to(vel[2 * q + 1, 0:1, :], (8, LANES))
        o1 = jnp.broadcast_to(vel[2 * q + 1, 1:2, :], (8, LANES))
        v = (
            jnp.where(low1, e0, pltpu.roll(o0, half, 1))[0:1],
            jnp.where(low1, pltpu.roll(e0, half, 1), o0)[0:1],
            jnp.where(low1, e1, o1)[0:1],
        )
        key_own = keys[q, 0, 0:1, :]
        key_next = keys[q, 1, 0:1, :]
        own = y_id == key_own
        nxt = y_id == key_next
        edge = edge_id == key_own
        v_edge = jnp.where(y_id < 2, v[0], jnp.where(y_id < 4, v[1], v[2]))
        parts = [jnp.where(own, v[c], 0.0) for c in range(3)]
        parts += [jnp.where(nxt, v[c], 0.0) for c in range(3)]
        parts += [jnp.where(edge, v_edge, 0.0)]
        cols = pl.ds(pl.multiple_of(q * LANES, LANES), LANES)
        for k, part in enumerate(parts):
            high = part.astype(jnp.bfloat16)
            rest = (part - high.astype(jnp.float32)).astype(jnp.bfloat16)
            lhs[k * cy : (k + 1) * cy, cols] = high
            lhs[n_row + k * cy : n_row + (k + 1) * cy, cols] = rest

    dot = lax.dot_general(
        lhs[...], zt[...], (((1,), (1,)), ((), ())), preferred_element_type=jnp.float32
    )
    face = dot[:n_row] + dot[n_row:]

    guarded(has[0], diag_copy.wait_recv)
    m_first, m_second, m_last = m_v[0], m_v[1], m_v[cx - 1]
    m_next = OMEGA / (6.0 + dgn_v[...])
    m_left = OMEGA / (6.0 + yrecv[0, 0, 3, 0:1, :])
    m_right = OMEGA / (6.0 + yrecv[0, 1, 3, 0:1, :])
    for c in (1, 0, 2):
        one = m_first * face[c * cy : (c + 1) * cy]
        one_next = m_next * face[(3 + c) * cy : (4 + c) * cy]
        base = 6 * cy + 2 * c
        left = m_left * face[base : base + 1]
        right = m_right * face[base + 1 : base + 2]
        add_first = (2.0 - OMEGA) * one + m_first * beside_plane(one, left, right)
        add_second = m_second * one
        add_last = m_last * one_next
        if c == 1:
            profile += circ_v[0] * add_first + circ_v[1] * add_second
            profile += circ_v[cx - 1] * add_last
            folded = sum(profile[:, k : k + LANES] for k in range(0, cz, LANES))
            folded = jnp.concatenate([folded, jnp.zeros((LANES - cy, LANES), jnp.float32)], axis=0)
            prof[b] = jnp.sum(folded.T, axis=0, keepdims=True)

            def prof_copy(dst, slot):
                return pltpu.make_async_remote_copy(
                    src_ref=prof.at[b],
                    dst_ref=prof.at[b],
                    send_sem=prof_send.at[slot],
                    recv_sem=prof_recv.at[b],
                    device_id=(dst, j),
                    device_id_type=MESH,
                )

            @pl.loop(1, n_blk)
            def _(i):
                prof_copy(lax.rem(b + i, n_blk), i).start()

        out_v[c, 0] += add_first
        out_v[c, 1] += add_second
        out_v[c, cx - 1] += add_last

    store_low = pltpu.make_async_copy(
        out_v.at[:, pl.ds(0, 2)], out_ref.at[:, pl.ds(0, 2)], sem_out.at[1]
    )
    store_high = pltpu.make_async_copy(
        out_v.at[:, pl.ds(cx - 1, 1)], out_ref.at[:, pl.ds(cx - 1, 1)], sem_out.at[2]
    )
    store_low.start()
    store_high.start()

    @pl.loop(1, n)
    def _(i):
        wake_copy(lax.rem(me + i, n), i).wait_send()
        vel_copy(lax.rem(me + i, n), i).wait_send()

    for k in range(4):
        guarded(has[k], halo0[k].wait_send)
        guarded(has[k], halo1[k].wait_send)
    guarded(has[1], diag_copy.wait_send)

    @pl.loop(1, n_blk)
    def _(i):
        src = lax.rem(b + n_blk - i, n_blk)
        pltpu.make_async_remote_copy(
            src_ref=prof.at[src],
            dst_ref=prof.at[src],
            send_sem=prof_send.at[i],
            recv_sem=prof_recv.at[src],
            device_id=(src, j),
            device_id_type=MESH,
        ).wait_recv()

    table = prof[:, 0, :].T
    place_id = seg_place.astype(jnp.int32)
    looked = jnp.zeros((cy, LANES), jnp.float32)
    for k in range(n_blk):
        looked += jnp.where(y_id + k * cy == place_id, table[:cy, k : k + 1], 0.0)
    looked = jnp.sum(looked, axis=0, keepdims=True)
    ng_ref[...] = (1.0 - RELAX) * gam_ref[...] + RELAX * looked
    store_ng = pltpu.make_async_copy(ng_ref, ng_hbm, sem_out.at[3])
    store_ng.start()

    @pl.loop(1, n_blk)
    def _(i):
        prof_copy(lax.rem(b + i, n_blk), i).wait_send()

    store_inner.wait()
    store_low.wait()
    store_high.wait()
    store_ng.wait()


def per_device(
    n_blk,
    n_bld,
    bnd_pos,
    bnd_owner,
    bnd_slot,
    seg_start,
    seg_step,
    seg_gamma,
    seg_sec,
    flow,
    source,
    extra_diag,
    circ_weight,
    sec_block,
    sec_row,
):
    n = n_blk * n_bld
    _, cx, cy, cz = flow.shape
    cells = bnd_pos.shape[1]
    half = cells // n_bld
    n_cells = n * half
    f32 = jnp.float32
    hbm = pl.BlockSpec(memory_space=pltpu.HBM)
    dma = pltpu.SemaphoreType.DMA
    return pl.pallas_call(
        functools.partial(kernel, n_blk, n_bld),
        out_shape=(
            jax.ShapeDtypeStruct(flow.shape, f32),
            jax.ShapeDtypeStruct(seg_gamma.shape, f32),
        ),
        in_specs=[hbm] * 13,
        out_specs=(hbm, hbm),
        scratch_shapes=[
            pltpu.VMEM(bnd_pos.shape, f32),
            pltpu.VMEM((cells // LANES, LANES), jnp.int32),
            pltpu.VMEM((cells // LANES, LANES), jnp.int32),
            pltpu.VMEM(seg_start.shape, f32),
            pltpu.VMEM(seg_step.shape, f32),
            pltpu.VMEM(seg_gamma.shape, f32),
            pltpu.VMEM(seg_sec.shape, jnp.int32),
            pltpu.VMEM(sec_block.shape, jnp.int32),
            pltpu.VMEM(sec_row.shape, jnp.int32),
            pltpu.VMEM(seg_gamma.shape, f32),
            pltpu.VMEM((n, 8, LANES), f32),
            pltpu.VMEM((n, 2, LANES), f32),
            pltpu.VMEM((n_blk, 1, LANES), f32),
            pltpu.VMEM((3, cx + 2, cy, cz), f32),
            pltpu.VMEM((3, cx + 2, cy, cz), f32),
            pltpu.VMEM((3, cx, cy, cz), f32),
            pltpu.VMEM((3, cx, cy, cz), f32),
            pltpu.VMEM((cx, cy, cz), f32),
            pltpu.VMEM((cx, cy, cz), f32),
            pltpu.VMEM((cx, cy, cz), f32),
            pltpu.VMEM((2, 2, 4, cx, cz), f32),
            pltpu.VMEM((2, 2, 4, cx, cz), f32),
            pltpu.VMEM((cy, cz), f32),
            pltpu.VMEM((8, cells), f32),
            pltpu.VMEM((cells, 8), f32),
            pltpu.VMEM((3, half, LANES), f32),
            pltpu.VMEM((n // 2, 2, 8, LANES), jnp.int32),
            pltpu.VMEM((cz, n_cells), jnp.bfloat16),
            pltpu.VMEM((14 * cy, n_cells), jnp.bfloat16),
            dma((13,)),
            dma((4,)),
            dma((n,)),
            dma((n,)),
            dma((n,)),
            dma((n,)),
            dma((n_blk,)),
            dma((n_blk,)),
            dma((9,)),
            dma((9,)),
        ],
        compiler_params=pltpu.CompilerParams(
            collective_id=0, has_side_effects=True, vmem_limit_bytes=56 * 1024 * 1024
        ),
    )(
        bnd_pos,
        bnd_owner.reshape(cells // LANES, LANES),
        bnd_slot.reshape(cells // LANES, LANES),
        seg_start,
        seg_step,
        seg_gamma,
        seg_sec,
        sec_block,
        sec_row,
        flow,
        source,
        extra_diag,
        circ_weight,
    )


def solution(mesh):
    return jax.shard_map(
        functools.partial(per_device, mesh.shape["blk"], mesh.shape["blade"]),
        mesh=mesh,
        in_specs=(
            P(None, "blk"),
            P("blk", None),
            P("blk"),
            P(None, "blade", "blk"),
            P(None, "blade", "blk"),
            P("blade", "blk"),
            P("blade", "blk"),
            P(None, "blk", "blade", None),
            P(None, "blk", "blade", None),
            P("blk", "blade", None),
            P("blk", "blade", None),
            P(),
            P(),
        ),
        out_specs=(P(None, "blk", "blade", None), P("blade", "blk")),
        check_vma=False,
    )
```

profile of v0, /device:TPU:0, one launch (start us, length us, event | category | flops | bytes accessed | tf_op | source)
XLA Modules:
  0.0 29.0 jit_solution(4089568618310386489)
XLA Ops:
  0.6 26.0 %shard_map.140 = (f32[3,8,16,256]{3,2,1,0:T(8,128)}, f32[1,128]{1,0:T(1,128)}) custom-call(f32[3,256]{1,0:T(4,128)} %pos_hbm.1, s32[2,128]{1,0:T(2,128)} %bitcast.2, s32[2,128]{1,0:T(2,128)} %bitcast.3, f32[3,1,128]{2,1,0:T(1,128)} %start_hbm.1, f32[3,1,128]{2,1,0:T(1,128)} %step_hbm.1, f32[1,128]{1,0:T(1,128)} %gam_hbm.1, s32[1,128]{1,0:T(1,128)} %sec_hbm.1, ...), custom_call_target="tpu_custom_call" | custom-call | tf_op jit(solution)/shard_map/pallas_call | solution.py:541
  26.7 0.0 copy-start
  26.7 1.8 %copy.17 = f32[3,8,16,256]{3,2,1,0:T(8,128)} copy(f32[3,8,16,256]{3,2,1,0:T(8,128)} %get-tuple-element.4) | data formatting | bytes 786432
  28.4 0.0 copy-done
  28.4 0.5 %copy.18 = f32[1,128]{1,0:T(1,128)} copy(f32[1,128]{1,0:T(1,128)S(1)} %copy-done) | data formatting | bytes 1024
Async XLA Ops:
  26.7 1.8 %copy-start = (f32[1,128]{1,0:T(1,128)S(1)}, f32[1,128]{1,0:T(1,128)}, u32[]{:S(2)}) copy-start(f32[1,128]{1,0:T(1,128)} %get-tuple-element.5) | copy-start | bytes 1540
where the time goes:
time: 29.1 us; the launch traced here: 29 us
  Pallas kernels  26 us (89%)
  local copies, waits for them, and re-layouts  2.28 us (8%)
  between operations  0.65 us (2%)
    pallas_call x1, Pallas kernels, per_device(): pl.pallas_call(functools.partial(kernel, n_blk, n_bld), out_shape=(jax.Sh...  26 us
    unnamed x4, local copies, waits for them, and re-layouts  2.28 us

commit v1 on v0

--- a/solution.py
+++ b/solution.py
@@ -32,8 +32,8 @@
     src_ref,
     diag_ref,
     circ_ref,
-    out_ref,
-    ng_hbm,
+    out_v,
+    ng_ref,
     pos_ref,
     own_ref,
     slot_ref,
@@ -43,13 +43,11 @@
     sec_ref,
     sblk_ref,
     srow_ref,
-    ng_ref,
     gath,
     vel,
     prof,
     flow_v,
     mid_v,
-    out_v,
     src_v,
     diag_v,
     circ_v,
@@ -64,7 +62,6 @@
     zt,
     lhs,
     sem_in,
-    sem_out,
     wake_send,
     wake_recv,
     vel_send,
@@ -363,11 +360,6 @@
         return total
 
     profile = lax.fori_loop(0, cx, second, jnp.zeros((cy, cz), jnp.float32))
-    store_inner = pltpu.make_async_copy(
-        out_v.at[:, pl.ds(2, cx - 3)], out_ref.at[:, pl.ds(2, cx - 3)], sem_out.at[0]
-    )
-    store_inner.start()
-
     z_id = lax.broadcasted_iota(jnp.int32, (cz, LANES), 0)
 
     @pl.loop(0, n_pair, unroll=4)
@@ -462,15 +454,6 @@
         out_v[c, 1] += add_second
         out_v[c, cx - 1] += add_last
 
-    store_low = pltpu.make_async_copy(
-        out_v.at[:, pl.ds(0, 2)], out_ref.at[:, pl.ds(0, 2)], sem_out.at[1]
-    )
-    store_high = pltpu.make_async_copy(
-        out_v.at[:, pl.ds(cx - 1, 1)], out_ref.at[:, pl.ds(cx - 1, 1)], sem_out.at[2]
-    )
-    store_low.start()
-    store_high.start()
-
     @pl.loop(1, n)
     def _(i):
         wake_copy(lax.rem(me + i, n), i).wait_send()
@@ -500,17 +483,22 @@
         looked += jnp.where(y_id + k * cy == place_id, table[:cy, k : k + 1], 0.0)
     looked = jnp.sum(looked, axis=0, keepdims=True)
     ng_ref[...] = (1.0 - RELAX) * gam_ref[...] + RELAX * looked
-    store_ng = pltpu.make_async_copy(ng_ref, ng_hbm, sem_out.at[3])
-    store_ng.start()
 
     @pl.loop(1, n_blk)
     def _(i):
         prof_copy(lax.rem(b + i, n_blk), i).wait_send()
 
-    store_inner.wait()
-    store_low.wait()
-    store_high.wait()
-    store_ng.wait()
+
+def hand_over(flow_v, gamma_v, flow_hbm, gamma_hbm, sem):
+    copies = [pltpu.make_async_copy(gamma_v, gamma_hbm, sem.at[0])]
+    copies += [
+        pltpu.make_async_copy(flow_v.at[c], flow_hbm.at[c], sem.at[1 + c])
+        for c in range(flow_v.shape[0])
+    ]
+    for copy in copies:
+        copy.start()
+    for copy in copies:
+        copy.wait()
 
 
 def per_device(
@@ -537,15 +525,16 @@
     n_cells = n * half
     f32 = jnp.float32
     hbm = pl.BlockSpec(memory_space=pltpu.HBM)
+    vmem = pl.BlockSpec(memory_space=pltpu.VMEM)
     dma = pltpu.SemaphoreType.DMA
-    return pl.pallas_call(
+    new_flow, new_gamma = pl.pallas_call(
         functools.partial(kernel, n_blk, n_bld),
         out_shape=(
-            jax.ShapeDtypeStruct(flow.shape, f32),
-            jax.ShapeDtypeStruct(seg_gamma.shape, f32),
+            pltpu.VMEM(flow.shape, f32),
+            pltpu.VMEM(seg_gamma.shape, f32),
         ),
         in_specs=[hbm] * 13,
-        out_specs=(hbm, hbm),
+        out_specs=(vmem, vmem),
         scratch_shapes=[
             pltpu.VMEM(bnd_pos.shape, f32),
             pltpu.VMEM((cells // LANES, LANES), jnp.int32),
@@ -556,13 +545,11 @@
             pltpu.VMEM(seg_sec.shape, jnp.int32),
             pltpu.VMEM(sec_block.shape, jnp.int32),
             pltpu.VMEM(sec_row.shape, jnp.int32),
-            pltpu.VMEM(seg_gamma.shape, f32),
             pltpu.VMEM((n, 8, LANES), f32),
             pltpu.VMEM((n, 2, LANES), f32),
             pltpu.VMEM((n_blk, 1, LANES), f32),
             pltpu.VMEM((3, cx + 2, cy, cz), f32),
             pltpu.VMEM((3, cx + 2, cy, cz), f32),
-            pltpu.VMEM((3, cx, cy, cz), f32),
             pltpu.VMEM((3, cx, cy, cz), f32),
             pltpu.VMEM((cx, cy, cz), f32),
             pltpu.VMEM((cx, cy, cz), f32),
@@ -577,7 +564,6 @@
             pltpu.VMEM((cz, n_cells), jnp.bfloat16),
             pltpu.VMEM((14 * cy, n_cells), jnp.bfloat16),
             dma((13,)),
-            dma((4,)),
             dma((n,)),
             dma((n,)),
             dma((n,)),
@@ -605,6 +591,19 @@
         extra_diag,
         circ_weight,
     )
+    return pl.pallas_call(
+        hand_over,
+        out_shape=(
+            jax.ShapeDtypeStruct(flow.shape, f32),
+            jax.ShapeDtypeStruct(seg_gamma.shape, f32),
+        ),
+        in_specs=[vmem, vmem],
+        out_specs=(hbm, hbm),
+        scratch_shapes=[dma((4,))],
+    )(
+        pltpu.with_memory_space_constraint(new_flow, pltpu.VMEM),
+        pltpu.with_memory_space_constraint(new_gamma, pltpu.VMEM),
+    )
 
 
 def solution(mesh):

time: 29.1 us -> 27 us (0.928)
  local copies, waits for them, and re-layouts: 2.28 us -> 0 us
    unnamed x4 -> x0, local copies, waits for them, and re-layouts: 2.28 us -> none
    pallas_call x1 -> x2, Pallas kernels: 26 us -> 26.2 us  [the longest x1 25.4 us: per_device(): pl.pallas_call(functools.partial(kernel, n_blk, n_bld), out_shape=(pltpu....]
where the time goes in v1:
time: 27 us; the launch traced here: 26.9 us
  Pallas kernels  26.2 us (97%)
  between operations  0.64 us (2%)
    pallas_call x1, Pallas kernels, per_device(): pl.pallas_call(functools.partial(kernel, n_blk, n_bld), out_shape=(pltpu....  25.4 us
    pallas_call x1, Pallas kernels, per_device(): pl.pallas_call(hand_over, out_shape=(jax.ShapeDtypeStruct(flow.shape, f32...  0.78 us

profile of v1, /device:TPU:0, one launch (start us, length us, event | category | flops | bytes accessed | tf_op | source)
XLA Modules:
  0.0 26.9 jit_solution(5398443721641560835)
XLA Ops:
  0.6 25.4 %shard_map.140 = (f32[3,8,16,256]{3,2,1,0:T(8,128)S(1)}, f32[1,128]{1,0:T(1,128)S(1)}) custom-call(f32[3,256]{1,0:T(4,128)} %pos_hbm.1, s32[2,128]{1,0:T(2,128)} %bitcast.2, s32[2,128]{1,0:T(2,128)} %bitcast.3, f32[3,1,128]{2,1,0:T(1,128)} %start_hbm.1, f32[3,1,128]{2,1,0:T(1,128)} %step_hbm.1, f32[1,128]{1,0:T(1,128)} %gam_hbm.1, s32[1,128]{1,0:T(1,128)} %sec_hbm.1, ...), custom_call_target="tpu_custom_call" | custom-call | tf_op jit(solution)/shard_map/pallas_call | solution.py:530
  26.1 0.8 %shard_map.141 = (f32[3,8,16,256]{3,2,1,0:T(8,128)}, f32[1,128]{1,0:T(1,128)}) custom-call(f32[3,8,16,256]{3,2,1,0:T(8,128)S(1)} %get-tuple-element.4.flow_v, f32[1,128]{1,0:T(1,128)S(1)} %get-tuple-element.5.gamma_v), custom_call_target="tpu_custom_call" | custom-call | tf_op jit(solution)/shard_map/pallas_call | solution.py:594

commit v2 on v1

--- a/solution.py
+++ b/solution.py
@@ -13,6 +13,7 @@
 OMEGA = 0.8
 RELAX = 0.5
 LANES = 128
+MIDDLE = 4
 MESH = pl.DeviceIdType.MESH
 
 
@@ -61,6 +62,9 @@
     keys,
     zt,
     lhs,
+    place_v,
+    share_v,
+    heed,
     sem_in,
     wake_send,
     wake_recv,
@@ -79,9 +83,46 @@
     half = pb.shape[1]
     n_pair = n // 2
     zbits = cz.bit_length() - 1
-
-    def dev(d):
+    flips = n & (n - 1) == 0 and n <= 64
+
+    def flip(a, mask, size):
+        bit = 1
+        out = a
+        while bit < size:
+            if mask & bit:
+                out = out + bit * (1 - 2 * lax.rem(lax.div(a, bit), 2))
+            bit *= 2
+        return out
+
+    def flip_dynamic(a, mask):
+        out, bit = 0, 1
+        while bit < n:
+            out = out + bit * lax.rem(lax.div(a, bit) + lax.div(mask, bit), 2)
+            bit *= 2
+        return out
+
+    def partners(limit, action):
+        if flips:
+            for i in range(limit - 1, 0, -1):
+                action(i)
+        else:
+            pl.loop(1, limit)(action)
+
+    def dev(i):
+        if flips:
+            return (flip(b, i // n_bld, n_blk), flip(j, i % n_bld, n_bld))
+        d = lax.rem(me + i, n)
         return (lax.div(d, n_bld), lax.rem(d, n_bld))
+
+    def blk_to(i):
+        return flip(b, i, n_blk) if flips else lax.rem(b + i, n_blk)
+
+    barrier = pltpu.get_barrier_semaphore()
+
+    def greet(i):
+        pl.semaphore_signal(barrier, inc=1, device_id=dev(i), device_id_type=MESH)
+
+    partners(n, greet)
 
     small = [
         pltpu.make_async_copy(source, target, sem_in.at[4 + k])
@@ -110,15 +151,7 @@
     for copy in loads:
         copy.start()
 
-    barrier = pltpu.get_barrier_semaphore()
-
-    @pl.loop(1, n)
-    def _(i):
-        pl.semaphore_signal(
-            barrier, inc=1, device_id=dev(lax.rem(me + i, n)), device_id_type=MESH
-        )
-
-    for copy in small:
+    for copy in small[:5]:
         copy.wait()
 
     lane1 = lax.broadcasted_iota(jnp.int32, (8, LANES), 1)
@@ -141,19 +174,17 @@
 
     pl.semaphore_wait(barrier, n - 1)
 
-    def wake_copy(dst, slot):
-        return pltpu.make_async_remote_copy(
+    def send_wake(i):
+        pltpu.make_async_remote_copy(
             src_ref=gath.at[me],
             dst_ref=gath.at[me],
-            send_sem=wake_send.at[slot],
+            send_sem=wake_send.at[0],
             recv_sem=wake_recv.at[me],
-            device_id=dev(dst),
+            device_id=dev(i),
             device_id_type=MESH,
-        )
-
-    @pl.loop(1, n)
-    def _(i):
-        wake_copy(lax.rem(me + i, n), i).start()
+        ).start()
+
+    partners(n, send_wake)
 
     has = (b < n_blk - 1, b > 0, j < n_bld - 1, j > 0)
     nxt_b, prv_b = (b + 1, j), (b - 1, j)
@@ -202,25 +233,6 @@
 
     arrives = (has[1], has[0], has[3], has[2])
 
-    @pl.when(b == 0)
-    def _():
-        flow_v[:, 0] = jnp.zeros((3, cy, cz), jnp.float32)
-        mid_v[:, 0] = jnp.zeros((3, cy, cz), jnp.float32)
-
-    @pl.when(b == n_blk - 1)
-    def _():
-        flow_v[:, cx + 1] = jnp.zeros((3, cy, cz), jnp.float32)
-        mid_v[:, cx + 1] = jnp.zeros((3, cy, cz), jnp.float32)
-        dgn_v[...] = jnp.zeros((cy, cz), jnp.float32)
-
-    @pl.when(j == 0)
-    def _():
-        yrecv[:, 0] = jnp.zeros(yrecv.shape[:1] + yrecv.shape[2:], jnp.float32)
-
-    @pl.when(j == n_bld - 1)
-    def _():
-        yrecv[:, 1] = jnp.zeros(yrecv.shape[:1] + yrecv.shape[2:], jnp.float32)
-
     loads[0].wait()
     loads[1].wait()
     for c in range(3):
@@ -232,6 +244,27 @@
     guarded(has[3], halo0[3].start)
     guarded(has[1], diag_copy.start)
 
+    @pl.when(b == 0)
+    def _():
+        flow_v[:, 0] = jnp.zeros((3, cy, cz), jnp.float32)
+        mid_v[:, 0] = jnp.zeros((3, cy, cz), jnp.float32)
+
+    @pl.when(b == n_blk - 1)
+    def _():
+        flow_v[:, cx + 1] = jnp.zeros((3, cy, cz), jnp.float32)
+        mid_v[:, cx + 1] = jnp.zeros((3, cy, cz), jnp.float32)
+        dgn_v[...] = jnp.zeros((cy, cz), jnp.float32)
+
+    @pl.when(j == 0)
+    def _():
+        yrecv[:, 0] = jnp.zeros(yrecv.shape[:1] + yrecv.shape[2:], jnp.float32)
+
+    @pl.when(j == n_bld - 1)
+    def _():
+        yrecv[:, 1] = jnp.zeros(yrecv.shape[:1] + yrecv.shape[2:], jnp.float32)
+
+    for copy in small[5:]:
+        copy.wait()
     pos8[...] = jnp.zeros(pos8.shape, jnp.float32)
     pos8[0:3, :] = pos_ref[...]
     post[...] = pos8[...].T
@@ -247,24 +280,51 @@
     )
     place = jnp.sum(jnp.where(eye, place, 0.0), axis=1, keepdims=True)
     match = lax.broadcasted_iota(jnp.int32, (n_sec, LANES), 0) == sec_ref[...]
-    seg_place = jnp.sum(jnp.where(match, place, 0.0), axis=0, keepdims=True)
+    place_v[0:1] = jnp.sum(jnp.where(match, place, 0.0), axis=0, keepdims=True)
 
     row_id = lax.broadcasted_iota(jnp.int32, (cy, cz), 0)
     col_id = lax.broadcasted_iota(jnp.int32, (cy, cz), 1)
+
+    def beside_lane(u):
+        total = jnp.where(col_id == 0, 0.0, pltpu.roll(u, 1, 1))
+        return total + jnp.where(col_id == cz - 1, 0.0, pltpu.roll(u, cz - 1, 1))
 
     def beside_plane(u, left, right):
         total = jnp.where(row_id == 0, left, pltpu.roll(u, 1, 0))
         total += jnp.where(row_id == cy - 1, right, pltpu.roll(u, cy - 1, 0))
-        total += jnp.where(col_id == 0, 0.0, pltpu.roll(u, 1, 1))
-        total += jnp.where(col_id == cz - 1, 0.0, pltpu.roll(u, cz - 1, 1))
-        return total
-
-    def relaxed(grid, stage, c, x, m):
-        u = grid[c, x + 1]
-        left = yrecv[stage, 0, c, pl.ds(x, 1), :]
-        right = yrecv[stage, 1, c, pl.ds(x, 1), :]
-        beside = beside_plane(u, left, right) + grid[c, x] + grid[c, x + 2]
-        return (1.0 - OMEGA) * u + m * (src_v[c, x] + beside)
+        return total + beside_lane(u)
+
+    def inside(grid, put):
+        def plane(x, sides):
+            m = m_v[x]
+            for c in range(3):
+                u = grid[c, x + 1]
+                beside = beside_plane(u, 0.0, 0.0)
+                for side in sides:
+                    beside += grid[c, x + 1 + side]
+                put(c, x, (1.0 - OMEGA) * u + m * (src_v[c, x] + beside))
+
+        plane(0, (1,))
+        pl.loop(1, cx - 1)(lambda x: plane(x, (-1, 1)))
+        plane(cx - 1, (-1,))
+
+    def edges(grid, stage, out, base):
+        for c in range(3):
+            out[c, base] += m_v[0] * grid[c, 0]
+            out[c, base + cx - 1] += m_v[cx - 1] * grid[c, cx + 1]
+            for side, row in ((0, 0), (1, cy - 1)):
+                out[c, base : base + cx, row, :] += m_v[:, row, :] * yrecv[stage, side, c]
+
+    @pl.loop(0, cx)
+    def _(x):
+        m_v[x] = OMEGA / (6.0 + diag_v[x])
+
+    loads[2].wait()
+
+    def put_mid(c, x, value):
+        mid_v[c, x + 1] = value
+
+    inside(flow_v, put_mid)
 
     def induce(src, acc):
         rows = [jnp.broadcast_to(gath[src, r : r + 1, :], (8, LANES)) for r in range(7)]
@@ -294,31 +354,23 @@
     acc = induce(me, (zero,) * (3 * (half // 8)))
 
     def wake_step(i, acc):
-        src = lax.rem(me + n - i, n)
+        src = flip_dynamic(me, i) if flips else lax.rem(me + n - i, n)
         pltpu.make_async_remote_copy(
             src_ref=gath.at[src],
             dst_ref=gath.at[src],
-            send_sem=wake_send.at[i],
+            send_sem=wake_send.at[0],
             recv_sem=wake_recv.at[src],
-            device_id=dev(src),
+            device_id=(lax.div(src, n_bld), lax.rem(src, n_bld)),
             device_id_type=MESH,
         ).wait_recv()
         return induce(src, acc)
 
-    middle = 5 * n // 8
+    middle = max(1, MIDDLE * n // 8)
     acc = lax.fori_loop(1, middle, wake_step, acc)
 
-    loads[2].wait()
     for k in range(4):
         guarded(arrives[k], halo0[k].wait_recv)
-
-    @pl.loop(0, cx)
-    def _(x):
-        m = OMEGA / (6.0 + diag_v[x])
-        m_v[x] = m
-        for c in range(3):
-            mid_v[c, x + 1] = relaxed(flow_v, 0, c, x, m)
-
+    edges(flow_v, 0, mid_v, 1)
     for c in range(3):
         ysend[1, 0, c] = mid_v[c, 1 : cx + 1, cy - 1, :]
         ysend[1, 1, c] = mid_v[c, 1 : cx + 1, 0, :]
@@ -329,38 +381,28 @@
 
     acc = lax.fori_loop(middle, n, wake_step, acc)
     ax, ay, az = (jnp.concatenate(acc[c::3], axis=0) for c in range(3))
-    vel[me, 0:1, :] = jnp.sum(jnp.concatenate([ax, ay], axis=0).T, axis=0, keepdims=True)
+    xy = jnp.sum(jnp.concatenate([ax, ay], axis=0).T, axis=0, keepdims=True)
+    yx = jnp.sum(jnp.concatenate([ay, ax], axis=0).T, axis=0, keepdims=True)
+    vel[me, 0:1, :] = jnp.where(mine_low, yx, xy)
     vel[me, 1:2, :] = jnp.sum(jnp.concatenate([az, az], axis=0).T, axis=0, keepdims=True)
 
-    def vel_copy(dst, slot):
-        return pltpu.make_async_remote_copy(
+    def send_vel(i):
+        pltpu.make_async_remote_copy(
             src_ref=vel.at[me],
             dst_ref=vel.at[me],
-            send_sem=vel_send.at[slot],
+            send_sem=vel_send.at[0],
             recv_sem=vel_recv.at[0],
-            device_id=dev(dst),
+            device_id=dev(i),
             device_id_type=MESH,
-        )
-
-    @pl.loop(1, n)
-    def _(i):
-        vel_copy(lax.rem(me + i, n), i).start()
-
-    loads[3].wait()
-    for k in range(4):
-        guarded(arrives[k], halo1[k].wait_recv)
-
-    def second(x, total):
-        m = m_v[x]
-        for c in range(3):
-            u = relaxed(mid_v, 1, c, x, m)
-            out_v[c, x] = u
-            if c == 1:
-                total += circ_v[x] * u
-        return total
-
-    profile = lax.fori_loop(0, cx, second, jnp.zeros((cy, cz), jnp.float32))
+        ).start()
+
+    partners(n, send_vel)
+
     z_id = lax.broadcasted_iota(jnp.int32, (cz, LANES), 0)
+    y_id = lax.broadcasted_iota(jnp.int32, (cy, LANES), 0)
+
+    def columns(q):
+        return pl.ds(pl.multiple_of(q * LANES, LANES), LANES)
 
     @pl.loop(0, n_pair, unroll=4)
     def _(q):
@@ -372,15 +414,84 @@
         col = slot & (cz - 1)
         keys[q, 0] = jnp.where(owner == b, row, -4 * cy * n_bld)
         keys[q, 1] = jnp.where(owner == b + 1, row, -4 * cy * n_bld)
-        cols = pl.ds(pl.multiple_of(q * LANES, LANES), LANES)
-        zt[:, cols] = jnp.where(z_id == col[0:1, :], 1.0, 0.0).astype(jnp.bfloat16)
-
-    y_id = lax.broadcasted_iota(jnp.int32, (cy, LANES), 0)
-    edge_id = jnp.where(y_id >= 6, -2, jnp.where((y_id & 1) == 0, -1, cy))
+        zt[:, columns(q)] = jnp.where(z_id == col[0:1, :], 1.0, 0.0).astype(jnp.bfloat16)
+
+    def put_out(c, x, value):
+        out_v[c, x] = value
+
+    inside(mid_v, put_out)
+
+    loads[3].wait()
+    guarded(has[0], diag_copy.wait_recv)
+    m_first, m_second, m_last = m_v[0], m_v[1], m_v[cx - 1]
+    m_next = OMEGA / (6.0 + dgn_v[...])
+    m_left = OMEGA / (6.0 + yrecv[0, 0, 3, 0:1, :])
+    m_right = OMEGA / (6.0 + yrecv[0, 1, 3, 0:1, :])
+    reach = circ_v[0] * m_first
+    share = jnp.concatenate(
+        [
+            m_first * ((2.0 - OMEGA) * circ_v[0] + m_second * circ_v[1] + beside_lane(reach)),
+            reach * jnp.where(row_id == 0, m_left, pltpu.roll(m_first, 1, 0)),
+            reach * jnp.where(row_id == cy - 1, m_right, pltpu.roll(m_first, cy - 1, 0)),
+            circ_v[cx - 1] * m_last * m_next,
+        ],
+        axis=0,
+    )
+    high = share.astype(jnp.bfloat16)
+    rest = (share - high.astype(jnp.float32)).astype(jnp.bfloat16)
+    share_v[0 : 4 * cy] = high
+    share_v[4 * cy : 8 * cy] = rest
+
+    @pl.loop(0, n_pair, unroll=2)
+    def _(q):
+        picked = jnp.dot(share_v[...], zt[:, columns(q)], preferred_element_type=jnp.float32)
+        picked = picked[: 4 * cy] + picked[4 * cy :]
+        key_own = keys[q, 0, 0:1, :]
+        key_next = keys[q, 1, 0:1, :]
+        total = jnp.where(y_id == key_own, picked[:cy], 0.0)
+        total += jnp.where(y_id - 1 == key_own, picked[cy : 2 * cy], 0.0)
+        total += jnp.where(y_id + 1 == key_own, picked[2 * cy : 3 * cy], 0.0)
+        total += jnp.where(y_id == key_next, picked[3 * cy :], 0.0)
+        heed[q] = total
+
+    for k in range(4):
+        guarded(arrives[k], halo1[k].wait_recv)
+    edges(mid_v, 1, out_v, 0)
+
+    profile = circ_v[0] * out_v[1, 0]
+    for x in range(1, cx):
+        profile += circ_v[x] * out_v[1, x]
+    profile = sum(profile[:, k : k + LANES] for k in range(0, cz, LANES))
 
     others = vel.at[pl.ds(0, n - 1)]
     pltpu.make_async_copy(others, others, vel_recv.at[0]).wait()
 
+    low_y = lax.broadcasted_iota(jnp.int32, (cy, LANES), 1) < half
+    for q in range(n_pair) if n_pair <= 32 else ():
+        v = jnp.where(low_y, vel[2 * q, 0:1, :], vel[2 * q + 1, 0:1, :])
+        profile += heed[q] * v
+    if n_pair > 32:
+
+        def heeded(q, total):
+            return total + heed[q] * jnp.where(low_y, vel[2 * q, 0:1, :], vel[2 * q + 1, 0:1, :])
+
+        profile = lax.fori_loop(0, n_pair, heeded, profile)
+    folded = jnp.concatenate([profile, jnp.zeros((LANES - cy, LANES), jnp.float32)], axis=0)
+    prof[b] = jnp.sum(folded.T, axis=0, keepdims=True)
+
+    def send_prof(i):
+        pltpu.make_async_remote_copy(
+            src_ref=prof.at[b],
+            dst_ref=prof.at[b],
+            send_sem=prof_send.at[0],
+            recv_sem=prof_recv.at[0],
+            device_id=(blk_to(i), j),
+            device_id_type=MESH,
+        ).start()
+
+    partners(n_blk, send_prof)
+
+    edge_id = jnp.where(y_id >= 6, -2, jnp.where((y_id & 1) == 0, -1, cy))
     n_row = 7 * cy
 
     @pl.loop(0, n_pair, unroll=4)
@@ -390,8 +501,8 @@
         o0 = jnp.broadcast_to(vel[2 * q + 1, 0:1, :], (8, LANES))
         o1 = jnp.broadcast_to(vel[2 * q + 1, 1:2, :], (8, LANES))
         v = (
-            jnp.where(low1, e0, pltpu.roll(o0, half, 1))[0:1],
-            jnp.where(low1, pltpu.roll(e0, half, 1), o0)[0:1],
+            pltpu.roll(jnp.where(low1, o0, e0), half, 1)[0:1],
+            jnp.where(low1, e0, o0)[0:1],
             jnp.where(low1, e1, o1)[0:1],
         )
         key_own = keys[q, 0, 0:1, :]
@@ -403,90 +514,45 @@
         parts = [jnp.where(own, v[c], 0.0) for c in range(3)]
         parts += [jnp.where(nxt, v[c], 0.0) for c in range(3)]
         parts += [jnp.where(edge, v_edge, 0.0)]
-        cols = pl.ds(pl.multiple_of(q * LANES, LANES), LANES)
         for k, part in enumerate(parts):
             high = part.astype(jnp.bfloat16)
             rest = (part - high.astype(jnp.float32)).astype(jnp.bfloat16)
-            lhs[k * cy : (k + 1) * cy, cols] = high
-            lhs[n_row + k * cy : n_row + (k + 1) * cy, cols] = rest
+            lhs[k * cy : (k + 1) * cy, columns(q)] = high
+            lhs[n_row + k * cy : n_row + (k + 1) * cy, columns(q)] = rest
 
     dot = lax.dot_general(
         lhs[...], zt[...], (((1,), (1,)), ((), ())), preferred_element_type=jnp.float32
     )
     face = dot[:n_row] + dot[n_row:]
 
-    guarded(has[0], diag_copy.wait_recv)
-    m_first, m_second, m_last = m_v[0], m_v[1], m_v[cx - 1]
-    m_next = OMEGA / (6.0 + dgn_v[...])
-    m_left = OMEGA / (6.0 + yrecv[0, 0, 3, 0:1, :])
-    m_right = OMEGA / (6.0 + yrecv[0, 1, 3, 0:1, :])
-    for c in (1, 0, 2):
-        one = m_first * face[c * cy : (c + 1) * cy]
-        one_next = m_next * face[(3 + c) * cy : (4 + c) * cy]
+    for c in range(3):
+        one = m_v[0] * face[c * cy : (c + 1) * cy]
         base = 6 * cy + 2 * c
         left = m_left * face[base : base + 1]
         right = m_right * face[base + 1 : base + 2]
-        add_first = (2.0 - OMEGA) * one + m_first * beside_plane(one, left, right)
-        add_second = m_second * one
-        add_last = m_last * one_next
-        if c == 1:
-            profile += circ_v[0] * add_first + circ_v[1] * add_second
-            profile += circ_v[cx - 1] * add_last
-            folded = sum(profile[:, k : k + LANES] for k in range(0, cz, LANES))
-            folded = jnp.concatenate([folded, jnp.zeros((LANES - cy, LANES), jnp.float32)], axis=0)
-            prof[b] = jnp.sum(folded.T, axis=0, keepdims=True)
-
-            def prof_copy(dst, slot):
-                return pltpu.make_async_remote_copy(
-                    src_ref=prof.at[b],
-                    dst_ref=prof.at[b],
-                    send_sem=prof_send.at[slot],
-                    recv_sem=prof_recv.at[b],
-                    device_id=(dst, j),
-                    device_id_type=MESH,
-                )
-
-            @pl.loop(1, n_blk)
-            def _(i):
-                prof_copy(lax.rem(b + i, n_blk), i).start()
-
-        out_v[c, 0] += add_first
-        out_v[c, 1] += add_second
-        out_v[c, cx - 1] += add_last
-
-    @pl.loop(1, n)
-    def _(i):
-        wake_copy(lax.rem(me + i, n), i).wait_send()
-        vel_copy(lax.rem(me + i, n), i).wait_send()
-
+        out_v[c, 0] += (2.0 - OMEGA) * one + m_v[0] * beside_plane(one, left, right)
+        out_v[c, 1] += m_v[1] * one
+        out_v[c, cx - 1] += m_v[cx - 1] * (m_next * face[(3 + c) * cy : (4 + c) * cy])
+
+    sent = gath.at[pl.ds(0, n - 1)]
+    pltpu.make_async_copy(sent, sent, wake_send.at[0]).wait()
+    pltpu.make_async_copy(others, others, vel_send.at[0]).wait()
     for k in range(4):
         guarded(has[k], halo0[k].wait_send)
         guarded(has[k], halo1[k].wait_send)
     guarded(has[1], diag_copy.wait_send)
 
-    @pl.loop(1, n_blk)
-    def _(i):
-        src = lax.rem(b + n_blk - i, n_blk)
-        pltpu.make_async_remote_copy(
-            src_ref=prof.at[src],
-            dst_ref=prof.at[src],
-            send_sem=prof_send.at[i],
-            recv_sem=prof_recv.at[src],
-            device_id=(src, j),
-            device_id_type=MESH,
-        ).wait_recv()
+    blocks = prof.at[pl.ds(0, n_blk - 1)]
+    pltpu.make_async_copy(blocks, blocks, prof_send.at[0]).wait()
+    pltpu.make_async_copy(blocks, blocks, prof_recv.at[0]).wait()
 
     table = prof[:, 0, :].T
-    place_id = seg_place.astype(jnp.int32)
+    place_id = place_v[0:1].astype(jnp.int32)
     looked = jnp.zeros((cy, LANES), jnp.float32)
     for k in range(n_blk):
         looked += jnp.where(y_id + k * cy == place_id, table[:cy, k : k + 1], 0.0)
     looked = jnp.sum(looked, axis=0, keepdims=True)
     ng_ref[...] = (1.0 - RELAX) * gam_ref[...] + RELAX * looked
-
-    @pl.loop(1, n_blk)
-    def _(i):
-        prof_copy(lax.rem(b + i, n_blk), i).wait_send()
 
 
 def hand_over(flow_v, gamma_v, flow_hbm, gamma_hbm, sem):
@@ -563,13 +629,16 @@
             pltpu.VMEM((n // 2, 2, 8, LANES), jnp.int32),
             pltpu.VMEM((cz, n_cells), jnp.bfloat16),
             pltpu.VMEM((14 * cy, n_cells), jnp.bfloat16),
+            pltpu.VMEM((8, LANES), f32),
+            pltpu.VMEM((8 * cy, cz), jnp.bfloat16),
+            pltpu.VMEM((n // 2, cy, LANES), f32),
             dma((13,)),
+            dma((1,)),
             dma((n,)),
-            dma((n,)),
-            dma((n,)),
-            dma((n,)),
-            dma((n_blk,)),
-            dma((n_blk,)),
+            dma((1,)),
+            dma((1,)),
+            dma((1,)),
+            dma((1,)),
             dma((9,)),
             dma((9,)),
         ],

time: 27 us -> 24.3 us (0.900)
  Pallas kernels: 26.2 us -> 23.5 us
    pallas_call x1, Pallas kernels: 25.4 us -> 22.7 us  [per_device(): pl.pallas_call(functools.partial(kernel, n_blk, n_bld), out_shape=(pltpu....]
where the time goes in v2:
time: 24.3 us; the launch traced here: 24.2 us
  Pallas kernels  23.5 us (97%)
  between operations  0.64 us (3%)
    pallas_call x1, Pallas kernels, per_device(): pl.pallas_call(functools.partial(kernel, n_blk, n_bld), out_shape=(pltpu....  22.7 us
    pallas_call x1, Pallas kernels, per_device(): pl.pallas_call(hand_over, out_shape=(jax.ShapeDtypeStruct(flow.shape, f32...  0.78 us

profile of v2, /device:TPU:0, one launch (start us, length us, event | category | flops | bytes accessed | tf_op | source)
XLA Modules:
  0.0 24.2 jit_solution(5979391958089151334)
XLA Ops:
  0.6 22.7 %shard_map.140 = (f32[3,8,16,256]{3,2,1,0:T(8,128)S(1)}, f32[1,128]{1,0:T(1,128)S(1)}) custom-call(f32[3,256]{1,0:T(4,128)} %pos_hbm.1, s32[2,128]{1,0:T(2,128)} %bitcast.2, s32[2,128]{1,0:T(2,128)} %bitcast.3, f32[3,1,128]{2,1,0:T(1,128)} %start_hbm.1, f32[3,1,128]{2,1,0:T(1,128)} %step_hbm.1, f32[1,128]{1,0:T(1,128)} %gam_hbm.1, s32[1,128]{1,0:T(1,128)} %sec_hbm.1, ...), custom_call_target="tpu_custom_call" | custom-call | tf_op jit(solution)/shard_map/pallas_call | solution.py:596
  23.4 0.8 %shard_map.141 = (f32[3,8,16,256]{3,2,1,0:T(8,128)}, f32[1,128]{1,0:T(1,128)}) custom-call(f32[3,8,16,256]{3,2,1,0:T(8,128)S(1)} %get-tuple-element.4.flow_v, f32[1,128]{1,0:T(1,128)S(1)} %get-tuple-element.5.gamma_v), custom_call_target="tpu_custom_call" | custom-call | tf_op jit(solution)/shard_map/pallas_call | solution.py:663

commit v3 on v2

--- a/solution.py
+++ b/solution.py
@@ -13,7 +13,7 @@
 OMEGA = 0.8
 RELAX = 0.5
 LANES = 128
-MIDDLE = 4
+MIDDLE = 5
 MESH = pl.DeviceIdType.MESH
 
 
@@ -65,7 +65,9 @@
     place_v,
     share_v,
     heed,
+    sums,
     sem_in,
+    tag_sem,
     wake_send,
     wake_recv,
     vel_send,
@@ -80,7 +82,6 @@
     j = lax.axis_index("blade")
     me = b * n_bld + j
     _, cx, cy, cz = src_v.shape
-    half = pb.shape[1]
     n_pair = n // 2
     zbits = cz.bit_length() - 1
     flips = n & (n - 1) == 0 and n <= 64
@@ -101,12 +102,12 @@
             bit *= 2
         return out
 
-    def partners(limit, action):
+    def partners(first, limit, action):
         if flips:
-            for i in range(limit - 1, 0, -1):
+            for i in range(limit - 1, first - 1, -1):
                 action(i)
         else:
-            pl.loop(1, limit)(action)
+            pl.loop(first, limit)(action)
 
     def dev(i):
         if flips:
@@ -122,7 +123,7 @@
     def greet(i):
         pl.semaphore_signal(barrier, inc=1, device_id=dev(i), device_id_type=MESH)
 
-    partners(n, greet)
+    partners(1, n, greet)
 
     small = [
         pltpu.make_async_copy(source, target, sem_in.at[4 + k])
@@ -154,23 +155,15 @@
     for copy in small[:5]:
         copy.wait()
 
-    lane1 = lax.broadcasted_iota(jnp.int32, (8, LANES), 1)
-    low1 = lane1 < half
-    slot_row = jnp.broadcast_to(
-        slot_ref[pl.ds(lax.div(j, 2), 1), :].astype(jnp.float32), (8, LANES)
-    )
-    own_row = jnp.broadcast_to(
-        own_ref[pl.ds(lax.div(j, 2), 1), :].astype(jnp.float32), (8, LANES)
-    )
-    mine_low = lax.rem(j, 2) == 0
-    own_row = pltpu.roll(own_row, half, 1)
-    first = jnp.where(low1, slot_row, own_row)
-    second = jnp.where(low1, own_row, slot_row)
-    tag = jnp.where(mine_low, first, second)
+    side = lax.rem(j, 2)
+    pair = lax.div(j, 2)
+    slot_row = slot_ref[pl.ds(pair, 1), :].astype(jnp.float32)
+    own_row = own_ref[pl.ds(pair, 1), :].astype(jnp.float32)
+    tag = jnp.where(side == 0, slot_row, own_row)
     gath[me, 0:3, :] = start_ref[:, 0, :]
     gath[me, 3:6, :] = step_ref[:, 0, :]
     gath[me, 6:7, :] = gam_ref[...]
-    gath[me, 7:8, :] = tag[0:1, :]
+    gath[me, 7:8, :] = tag
 
     pl.semaphore_wait(barrier, n - 1)
 
@@ -180,11 +173,22 @@
             dst_ref=gath.at[me],
             send_sem=wake_send.at[0],
             recv_sem=wake_recv.at[me],
-            device_id=dev(i),
+            device_id=dev(2 * i),
             device_id_type=MESH,
         ).start()
 
-    partners(n, send_wake)
+    def send_tag(i):
+        pltpu.make_async_remote_copy(
+            src_ref=gath.at[me, pl.ds(7, 1)],
+            dst_ref=gath.at[me, pl.ds(7, 1)],
+            send_sem=tag_sem.at[0],
+            recv_sem=tag_sem.at[1],
+            device_id=dev(2 * i + 1),
+            device_id_type=MESH,
+        ).start()
+
+    partners(1, n // 2, send_wake)
+    partners(0, n // 2, send_tag)
 
     has = (b < n_blk - 1, b > 0, j < n_bld - 1, j > 0)
     nxt_b, prv_b = (b + 1, j), (b - 1, j)
@@ -268,9 +272,9 @@
     pos8[...] = jnp.zeros(pos8.shape, jnp.float32)
     pos8[0:3, :] = pos_ref[...]
     post[...] = pos8[...].T
-    mine = post[pl.ds(pl.multiple_of(j * half, half), half), :]
+    mine = post[pl.ds(pl.multiple_of(pair * LANES, LANES), LANES), :]
     for c in range(3):
-        pb[c] = jnp.broadcast_to(mine[:, c : c + 1], (half, LANES))
+        pb[c] = jnp.broadcast_to(mine[:, c : c + 1], (LANES, LANES))
 
     n_sec = sblk_ref.shape[1]
     place = sblk_ref[pl.ds(j, 1), :] * cy + srow_ref[pl.ds(j, 1), :]
@@ -326,14 +330,13 @@
 
     inside(flow_v, put_mid)
 
-    def induce(src, acc):
+    def induce(src, first):
         rows = [jnp.broadcast_to(gath[src, r : r + 1, :], (8, LANES)) for r in range(7)]
         sx, sy, sz, dx, dy, dz, gam = rows
         dd = dx * dx + dy * dy + dz * dz
         bias = CORE * dd + CORE * CORE
         gam = gam * (1.0 / FOUR_PI)
-        acc = list(acc)
-        for g in range(half // 8):
+        for g in range(LANES // 8):
             part = slice(8 * g, 8 * g + 8)
             rx, ry, rz = pb[0, part] - sx, pb[1, part] - sy, pb[2, part] - sz
             along_one = dx * rx + dy * ry + dz * rz
@@ -345,16 +348,16 @@
             ky = dz * rx - dx * rz
             kz = dx * ry - dy * rx
             w = gam * along / (kx * kx + ky * ky + kz * kz + bias)
-            acc[3 * g] += w * kx
-            acc[3 * g + 1] += w * ky
-            acc[3 * g + 2] += w * kz
-        return tuple(acc)
-
-    zero = jnp.zeros((8, LANES), jnp.float32)
-    acc = induce(me, (zero,) * (3 * (half // 8)))
-
-    def wake_step(i, acc):
-        src = flip_dynamic(me, i) if flips else lax.rem(me + n - i, n)
+            for c, k in enumerate((kx, ky, kz)):
+                if first:
+                    sums[c, part] = w * k
+                else:
+                    sums[c, part] += w * k
+
+    induce(me, True)
+
+    def wake_step(i):
+        src = flip_dynamic(me, 2 * i) if flips else lax.rem(me + n - 2 * i, n)
         pltpu.make_async_remote_copy(
             src_ref=gath.at[src],
             dst_ref=gath.at[src],
@@ -363,10 +366,10 @@
             device_id=(lax.div(src, n_bld), lax.rem(src, n_bld)),
             device_id_type=MESH,
         ).wait_recv()
-        return induce(src, acc)
-
-    middle = max(1, MIDDLE * n // 8)
-    acc = lax.fori_loop(1, middle, wake_step, acc)
+        induce(src, False)
+
+    middle = max(1, MIDDLE * n // 16)
+    pl.loop(1, middle)(wake_step)
 
     for k in range(4):
         guarded(arrives[k], halo0[k].wait_recv)
@@ -379,12 +382,9 @@
     for k in range(4):
         guarded(has[k], halo1[k].start)
 
-    acc = lax.fori_loop(middle, n, wake_step, acc)
-    ax, ay, az = (jnp.concatenate(acc[c::3], axis=0) for c in range(3))
-    xy = jnp.sum(jnp.concatenate([ax, ay], axis=0).T, axis=0, keepdims=True)
-    yx = jnp.sum(jnp.concatenate([ay, ax], axis=0).T, axis=0, keepdims=True)
-    vel[me, 0:1, :] = jnp.where(mine_low, yx, xy)
-    vel[me, 1:2, :] = jnp.sum(jnp.concatenate([az, az], axis=0).T, axis=0, keepdims=True)
+    pl.loop(middle, n // 2)(wake_step)
+    for c in range(3):
+        vel[me, c : c + 1, :] = jnp.sum(sums[c].T, axis=0, keepdims=True)
 
     def send_vel(i):
         pltpu.make_async_remote_copy(
@@ -396,7 +396,10 @@
             device_id_type=MESH,
         ).start()
 
-    partners(n, send_vel)
+    partners(1, n, send_vel)
+
+    tags = gath.at[pl.ds(0, n // 16)]
+    pltpu.make_async_copy(tags, tags, tag_sem.at[1]).wait()
 
     z_id = lax.broadcasted_iota(jnp.int32, (cz, LANES), 0)
     y_id = lax.broadcasted_iota(jnp.int32, (cy, LANES), 0)
@@ -406,10 +409,8 @@
 
     @pl.loop(0, n_pair, unroll=4)
     def _(q):
-        even = jnp.broadcast_to(gath[2 * q, 7:8, :], (8, LANES))
-        odd = jnp.broadcast_to(gath[2 * q + 1, 7:8, :], (8, LANES))
-        slot = jnp.where(low1, even, odd).astype(jnp.int32)
-        owner = pltpu.roll(jnp.where(low1, odd, even), half, 1).astype(jnp.int32)
+        slot = jnp.broadcast_to(gath[2 * q, 7:8, :], (8, LANES)).astype(jnp.int32)
+        owner = jnp.broadcast_to(gath[2 * q + 1, 7:8, :], (8, LANES)).astype(jnp.int32)
         row = (slot >> zbits) - j * cy
         col = slot & (cz - 1)
         keys[q, 0] = jnp.where(owner == b, row, -4 * cy * n_bld)
@@ -466,15 +467,13 @@
     others = vel.at[pl.ds(0, n - 1)]
     pltpu.make_async_copy(others, others, vel_recv.at[0]).wait()
 
-    low_y = lax.broadcasted_iota(jnp.int32, (cy, LANES), 1) < half
-    for q in range(n_pair) if n_pair <= 32 else ():
-        v = jnp.where(low_y, vel[2 * q, 0:1, :], vel[2 * q + 1, 0:1, :])
-        profile += heed[q] * v
-    if n_pair > 32:
-
-        def heeded(q, total):
-            return total + heed[q] * jnp.where(low_y, vel[2 * q, 0:1, :], vel[2 * q + 1, 0:1, :])
-
+    def heeded(q, total):
+        return total + heed[q] * (vel[2 * q, 1:2, :] + vel[2 * q + 1, 1:2, :])
+
+    if n_pair <= 32:
+        for q in range(n_pair):
+            profile = heeded(q, profile)
+    else:
         profile = lax.fori_loop(0, n_pair, heeded, profile)
     folded = jnp.concatenate([profile, jnp.zeros((LANES - cy, LANES), jnp.float32)], axis=0)
     prof[b] = jnp.sum(folded.T, axis=0, keepdims=True)
@@ -489,22 +488,14 @@
             device_id_type=MESH,
         ).start()
 
-    partners(n_blk, send_prof)
+    partners(1, n_blk, send_prof)
 
     edge_id = jnp.where(y_id >= 6, -2, jnp.where((y_id & 1) == 0, -1, cy))
     n_row = 7 * cy
 
     @pl.loop(0, n_pair, unroll=4)
     def _(q):
-        e0 = jnp.broadcast_to(vel[2 * q, 0:1, :], (8, LANES))
-        e1 = jnp.broadcast_to(vel[2 * q, 1:2, :], (8, LANES))
-        o0 = jnp.broadcast_to(vel[2 * q + 1, 0:1, :], (8, LANES))
-        o1 = jnp.broadcast_to(vel[2 * q + 1, 1:2, :], (8, LANES))
-        v = (
-            pltpu.roll(jnp.where(low1, o0, e0), half, 1)[0:1],
-            jnp.where(low1, e0, o0)[0:1],
-            jnp.where(low1, e1, o1)[0:1],
-        )
+        v = tuple(vel[2 * q, c : c + 1, :] + vel[2 * q + 1, c : c + 1, :] for c in range(3))
         key_own = keys[q, 0, 0:1, :]
         key_next = keys[q, 1, 0:1, :]
         own = y_id == key_own
@@ -534,8 +525,9 @@
         out_v[c, 1] += m_v[1] * one
         out_v[c, cx - 1] += m_v[cx - 1] * (m_next * face[(3 + c) * cy : (4 + c) * cy])
 
-    sent = gath.at[pl.ds(0, n - 1)]
+    sent = gath.at[pl.ds(0, n // 2 - 1)]
     pltpu.make_async_copy(sent, sent, wake_send.at[0]).wait()
+    pltpu.make_async_copy(tags, tags, tag_sem.at[0]).wait()
     pltpu.make_async_copy(others, others, vel_send.at[0]).wait()
     for k in range(4):
         guarded(has[k], halo0[k].wait_send)
@@ -587,8 +579,7 @@
     n = n_blk * n_bld
     _, cx, cy, cz = flow.shape
     cells = bnd_pos.shape[1]
-    half = cells // n_bld
-    n_cells = n * half
+    n_cells = n_blk * cells
     f32 = jnp.float32
     hbm = pl.BlockSpec(memory_space=pltpu.HBM)
     vmem = pl.BlockSpec(memory_space=pltpu.VMEM)
@@ -612,7 +603,7 @@
             pltpu.VMEM(sec_block.shape, jnp.int32),
             pltpu.VMEM(sec_row.shape, jnp.int32),
             pltpu.VMEM((n, 8, LANES), f32),
-            pltpu.VMEM((n, 2, LANES), f32),
+            pltpu.VMEM((n, 3, LANES), f32),
             pltpu.VMEM((n_blk, 1, LANES), f32),
             pltpu.VMEM((3, cx + 2, cy, cz), f32),
             pltpu.VMEM((3, cx + 2, cy, cz), f32),
@@ -625,14 +616,16 @@
             pltpu.VMEM((cy, cz), f32),
             pltpu.VMEM((8, cells), f32),
             pltpu.VMEM((cells, 8), f32),
-            pltpu.VMEM((3, half, LANES), f32),
+            pltpu.VMEM((3, LANES, LANES), f32),
             pltpu.VMEM((n // 2, 2, 8, LANES), jnp.int32),
             pltpu.VMEM((cz, n_cells), jnp.bfloat16),
             pltpu.VMEM((14 * cy, n_cells), jnp.bfloat16),
             pltpu.VMEM((8, LANES), f32),
             pltpu.VMEM((8 * cy, cz), jnp.bfloat16),
             pltpu.VMEM((n // 2, cy, LANES), f32),
+            pltpu.VMEM((3, LANES, LANES), f32),
             dma((13,)),
+            dma((2,)),
             dma((1,)),
             dma((n,)),
             dma((1,)),

time: 24.3 us -> 23.5 us (0.967)
  Pallas kernels: 23.5 us -> 22.7 us
    pallas_call x1, Pallas kernels: 22.7 us -> 21.9 us  [per_device(): pl.pallas_call(functools.partial(kernel, n_blk, n_bld), out_shape=(pltpu....]
where the time goes in v3:
time: 23.5 us; the launch traced here: 23.3 us
  Pallas kernels  22.7 us (97%)
  between operations  0.64 us (3%)
    pallas_call x1, Pallas kernels, per_device(): pl.pallas_call(functools.partial(kernel, n_blk, n_bld), out_shape=(pltpu....  21.9 us
    pallas_call x1, Pallas kernels, per_device(): pl.pallas_call(hand_over, out_shape=(jax.ShapeDtypeStruct(flow.shape, f32...  0.78 us

profile of v3, /device:TPU:0, one launch (start us, length us, event | category | flops | bytes accessed | tf_op | source)
XLA Modules:
  0.0 23.3 jit_solution(9578310534118490358)
XLA Ops:
  0.6 21.9 %shard_map.140 = (f32[3,8,16,256]{3,2,1,0:T(8,128)S(1)}, f32[1,128]{1,0:T(1,128)S(1)}) custom-call(f32[3,256]{1,0:T(4,128)} %pos_hbm.1, s32[2,128]{1,0:T(2,128)} %bitcast.2, s32[2,128]{1,0:T(2,128)} %bitcast.3, f32[3,1,128]{2,1,0:T(1,128)} %start_hbm.1, f32[3,1,128]{2,1,0:T(1,128)} %step_hbm.1, f32[1,128]{1,0:T(1,128)} %gam_hbm.1, s32[1,128]{1,0:T(1,128)} %sec_hbm.1, ...), custom_call_target="tpu_custom_call" | custom-call | tf_op jit(solution)/shard_map/pallas_call | solution.py:587
  22.6 0.8 %shard_map.141 = (f32[3,8,16,256]{3,2,1,0:T(8,128)}, f32[1,128]{1,0:T(1,128)}) custom-call(f32[3,8,16,256]{3,2,1,0:T(8,128)S(1)} %get-tuple-element.4.flow_v, f32[1,128]{1,0:T(1,128)S(1)} %get-tuple-element.5.gamma_v), custom_call_target="tpu_custom_call" | custom-call | tf_op jit(solution)/shard_map/pallas_call | solution.py:656

commit v4 on v3

--- a/solution.py
+++ b/solution.py
@@ -13,7 +13,6 @@
 OMEGA = 0.8
 RELAX = 0.5
 LANES = 128
-MIDDLE = 5
 MESH = pl.DeviceIdType.MESH
 
 
@@ -36,14 +35,11 @@
     out_v,
     ng_ref,
     pos_ref,
-    own_ref,
-    slot_ref,
-    start_ref,
-    step_ref,
+    tag_ref,
+    line_ref,
     gam_ref,
     sec_ref,
-    sblk_ref,
-    srow_ref,
+    sect_ref,
     gath,
     vel,
     prof,
@@ -126,23 +122,25 @@
     partners(1, n, greet)
 
     small = [
-        pltpu.make_async_copy(source, target, sem_in.at[4 + k])
-        for k, (source, target) in enumerate(
-            (
-                (start_hbm, start_ref),
-                (step_hbm, step_ref),
-                (gam_hbm, gam_ref),
-                (slot_hbm, slot_ref),
-                (own_hbm, own_ref),
-                (pos_hbm, pos_ref),
-                (sec_hbm, sec_ref),
-                (sblk_hbm, sblk_ref),
-                (srow_hbm, srow_ref),
-            )
+        pltpu.make_async_copy(source, target, sem_in.at[k])
+        for k, source, target in (
+            (4, start_hbm, line_ref.at[0]),
+            (4, step_hbm, line_ref.at[1]),
+            (5, gam_hbm, gam_ref),
+            (6, slot_hbm, tag_ref.at[0]),
+            (6, own_hbm, tag_ref.at[1]),
+            (7, pos_hbm, pos_ref),
+            (8, sec_hbm, sec_ref),
+            (9, sblk_hbm, sect_ref.at[0]),
+            (9, srow_hbm, sect_ref.at[1]),
         )
     ]
     for copy in small:
         copy.start()
+
+    def landed(ref, k):
+        pltpu.make_async_copy(ref, ref, sem_in.at[k]).wait()
+
     loads = [
         pltpu.make_async_copy(flow_ref, flow_v.at[:, pl.ds(1, cx)], sem_in.at[0]),
         pltpu.make_async_copy(diag_ref, diag_v, sem_in.at[1]),
@@ -152,16 +150,17 @@
     for copy in loads:
         copy.start()
 
-    for copy in small[:5]:
-        copy.wait()
+    landed(line_ref, 4)
+    landed(gam_ref, 5)
+    landed(tag_ref, 6)
 
     side = lax.rem(j, 2)
     pair = lax.div(j, 2)
-    slot_row = slot_ref[pl.ds(pair, 1), :].astype(jnp.float32)
-    own_row = own_ref[pl.ds(pair, 1), :].astype(jnp.float32)
+    slot_row = tag_ref[0, pl.ds(pair, 1), :].astype(jnp.float32)
+    own_row = tag_ref[1, pl.ds(pair, 1), :].astype(jnp.float32)
     tag = jnp.where(side == 0, slot_row, own_row)
-    gath[me, 0:3, :] = start_ref[:, 0, :]
-    gath[me, 3:6, :] = step_ref[:, 0, :]
+    gath[me, 0:3, :] = line_ref[0, :, 0, :]
+    gath[me, 3:6, :] = line_ref[1, :, 0, :]
     gath[me, 6:7, :] = gam_ref[...]
     gath[me, 7:8, :] = tag
 
@@ -172,7 +171,7 @@
             src_ref=gath.at[me],
             dst_ref=gath.at[me],
             send_sem=wake_send.at[0],
-            recv_sem=wake_recv.at[me],
+            recv_sem=wake_recv.at[i // 2],
             device_id=dev(2 * i),
             device_id_type=MESH,
         ).start()
@@ -267,8 +266,9 @@
     def _():
         yrecv[:, 1] = jnp.zeros(yrecv.shape[:1] + yrecv.shape[2:], jnp.float32)
 
-    for copy in small[5:]:
-        copy.wait()
+    landed(pos_ref, 7)
+    landed(sec_ref, 8)
+    landed(sect_ref, 9)
     pos8[...] = jnp.zeros(pos8.shape, jnp.float32)
     pos8[0:3, :] = pos_ref[...]
     post[...] = pos8[...].T
@@ -276,8 +276,8 @@
     for c in range(3):
         pb[c] = jnp.broadcast_to(mine[:, c : c + 1], (LANES, LANES))
 
-    n_sec = sblk_ref.shape[1]
-    place = sblk_ref[pl.ds(j, 1), :] * cy + srow_ref[pl.ds(j, 1), :]
+    n_sec = sect_ref.shape[2]
+    place = sect_ref[0, pl.ds(j, 1), :] * cy + sect_ref[1, pl.ds(j, 1), :]
     place = jnp.broadcast_to(place.astype(jnp.float32), (n_sec, n_sec))
     eye = lax.broadcasted_iota(jnp.int32, (n_sec, n_sec), 0) == lax.broadcasted_iota(
         jnp.int32, (n_sec, n_sec), 1
@@ -356,21 +356,36 @@
 
     induce(me, True)
 
-    def wake_step(i):
-        src = flip_dynamic(me, 2 * i) if flips else lax.rem(me + n - 2 * i, n)
+    def wake_wait(k, count):
+        came = gath.at[pl.ds(0, count)]
+        pltpu.make_async_copy(came, came, wake_recv.at[k]).wait()
+
+    def wake_from(i):
+        induce(flip_dynamic(me, 2 * i) if flips else lax.rem(me + n - 2 * i, n), False)
+
+    wake_wait(0, 1)
+    wake_from(1)
+
+    @pl.loop(1, n // 4)
+    def _(k):
+        wake_wait(k, 2)
+        wake_from(2 * k)
+        wake_from(2 * k + 1)
+
+    for c in range(3):
+        vel[me, c : c + 1, :] = jnp.sum(sums[c].T, axis=0, keepdims=True)
+
+    def send_vel(i):
         pltpu.make_async_remote_copy(
-            src_ref=gath.at[src],
-            dst_ref=gath.at[src],
-            send_sem=wake_send.at[0],
-            recv_sem=wake_recv.at[src],
-            device_id=(lax.div(src, n_bld), lax.rem(src, n_bld)),
+            src_ref=vel.at[me],
+            dst_ref=vel.at[me],
+            send_sem=vel_send.at[0],
+            recv_sem=vel_recv.at[0],
+            device_id=dev(i),
             device_id_type=MESH,
-        ).wait_recv()
-        induce(src, False)
-
-    middle = max(1, MIDDLE * n // 16)
-    pl.loop(1, middle)(wake_step)
-
+        ).start()
+
+    partners(1, n, send_vel)
     for k in range(4):
         guarded(arrives[k], halo0[k].wait_recv)
     edges(flow_v, 0, mid_v, 1)
@@ -382,21 +397,6 @@
     for k in range(4):
         guarded(has[k], halo1[k].start)
 
-    pl.loop(middle, n // 2)(wake_step)
-    for c in range(3):
-        vel[me, c : c + 1, :] = jnp.sum(sums[c].T, axis=0, keepdims=True)
-
-    def send_vel(i):
-        pltpu.make_async_remote_copy(
-            src_ref=vel.at[me],
-            dst_ref=vel.at[me],
-            send_sem=vel_send.at[0],
-            recv_sem=vel_recv.at[0],
-            device_id=dev(i),
-            device_id_type=MESH,
-        ).start()
-
-    partners(1, n, send_vel)
 
     tags = gath.at[pl.ds(0, n // 16)]
     pltpu.make_async_copy(tags, tags, tag_sem.at[1]).wait()
@@ -594,14 +594,11 @@
         out_specs=(vmem, vmem),
         scratch_shapes=[
             pltpu.VMEM(bnd_pos.shape, f32),
-            pltpu.VMEM((cells // LANES, LANES), jnp.int32),
-            pltpu.VMEM((cells // LANES, LANES), jnp.int32),
-            pltpu.VMEM(seg_start.shape, f32),
-            pltpu.VMEM(seg_step.shape, f32),
+            pltpu.VMEM((2, cells // LANES, LANES), jnp.int32),
+            pltpu.VMEM((2, *seg_start.shape), f32),
             pltpu.VMEM(seg_gamma.shape, f32),
             pltpu.VMEM(seg_sec.shape, jnp.int32),
-            pltpu.VMEM(sec_block.shape, jnp.int32),
-            pltpu.VMEM(sec_row.shape, jnp.int32),
+            pltpu.VMEM((2, *sec_block.shape), jnp.int32),
             pltpu.VMEM((n, 8, LANES), f32),
             pltpu.VMEM((n, 3, LANES), f32),
             pltpu.VMEM((n_blk, 1, LANES), f32),
@@ -624,10 +621,10 @@
             pltpu.VMEM((8 * cy, cz), jnp.bfloat16),
             pltpu.VMEM((n // 2, cy, LANES), f32),
             pltpu.VMEM((3, LANES, LANES), f32),
-            dma((13,)),
+            dma((10,)),
             dma((2,)),
             dma((1,)),
-            dma((n,)),
+            dma((n // 4,)),
             dma((1,)),
             dma((1,)),
             dma((1,)),

time: 23.5 us -> 22.4 us (0.953)
  Pallas kernels: 22.7 us -> 21.6 us
    pallas_call x1, Pallas kernels: 21.9 us -> 20.8 us  [per_device(): pl.pallas_call(functools.partial(kernel, n_blk, n_bld), out_shape=(pltpu....]
where the time goes in v4:
time: 22.4 us; the launch traced here: 22.3 us
  Pallas kernels  21.6 us (96%)
  between operations  0.64 us (3%)
    pallas_call x1, Pallas kernels, per_device(): pl.pallas_call(functools.partial(kernel, n_blk, n_bld), out_shape=(pltpu....  20.8 us
    pallas_call x1, Pallas kernels, per_device(): pl.pallas_call(hand_over, out_shape=(jax.ShapeDtypeStruct(flow.shape, f32...  0.78 us

profile of v4, /device:TPU:0, one launch (start us, length us, event | category | flops | bytes accessed | tf_op | source)
XLA Modules:
  0.0 22.3 jit_solution(16140436675062169538)
XLA Ops:
  0.6 20.8 %shard_map.140 = (f32[3,8,16,256]{3,2,1,0:T(8,128)S(1)}, f32[1,128]{1,0:T(1,128)S(1)}) custom-call(f32[3,256]{1,0:T(4,128)} %pos_hbm.1, s32[2,128]{1,0:T(2,128)} %bitcast.2, s32[2,128]{1,0:T(2,128)} %bitcast.3, f32[3,1,128]{2,1,0:T(1,128)} %start_hbm.1, f32[3,1,128]{2,1,0:T(1,128)} %step_hbm.1, f32[1,128]{1,0:T(1,128)} %gam_hbm.1, s32[1,128]{1,0:T(1,128)} %sec_hbm.1, ...), custom_call_target="tpu_custom_call" | custom-call | tf_op jit(solution)/shard_map/pallas_call | solution.py:587
  21.5 0.8 %shard_map.141 = (f32[3,8,16,256]{3,2,1,0:T(8,128)}, f32[1,128]{1,0:T(1,128)}) custom-call(f32[3,8,16,256]{3,2,1,0:T(8,128)S(1)} %get-tuple-element.4.flow_v, f32[1,128]{1,0:T(1,128)S(1)} %get-tuple-element.5.gamma_v), custom_call_target="tpu_custom_call" | custom-call | tf_op jit(solution)/shard_map/pallas_call | solution.py:653

commit v5 on v4

--- a/solution.py
+++ b/solution.py
@@ -13,6 +13,7 @@
 OMEGA = 0.8
 RELAX = 0.5
 LANES = 128
+EARLY = 6
 MESH = pl.DeviceIdType.MESH
 
 
@@ -62,7 +63,15 @@
     share_v,
     heed,
     sums,
+    mask_v,
+    spot_v,
+    near_v,
+    coef_v,
+    name_v,
+    line_v,
+    msg,
     sem_in,
+    msg_sem,
     tag_sem,
     wake_send,
     wake_recv,
@@ -80,6 +89,8 @@
     _, cx, cy, cz = src_v.shape
     n_pair = n // 2
     zbits = cz.bit_length() - 1
+    cap = LANES // 2
+    compact = n_blk == 8 and n_bld == 4
     flips = n & (n - 1) == 0 and n <= 64
 
     def flip(a, mask, size):
@@ -366,26 +377,14 @@
     wake_wait(0, 1)
     wake_from(1)
 
-    @pl.loop(1, n // 4)
-    def _(k):
+    def wake_pair(k):
         wake_wait(k, 2)
         wake_from(2 * k)
         wake_from(2 * k + 1)
 
-    for c in range(3):
-        vel[me, c : c + 1, :] = jnp.sum(sums[c].T, axis=0, keepdims=True)
-
-    def send_vel(i):
-        pltpu.make_async_remote_copy(
-            src_ref=vel.at[me],
-            dst_ref=vel.at[me],
-            send_sem=vel_send.at[0],
-            recv_sem=vel_recv.at[0],
-            device_id=dev(i),
-            device_id_type=MESH,
-        ).start()
-
-    partners(1, n, send_vel)
+    early = max(1, EARLY * n // 32)
+    pl.loop(1, early)(wake_pair)
+
     for k in range(4):
         guarded(arrives[k], halo0[k].wait_recv)
     edges(flow_v, 0, mid_v, 1)
@@ -398,6 +397,22 @@
         guarded(has[k], halo1[k].start)
 
 
+    pl.loop(early, n // 4)(wake_pair)
+    for c in range(3):
+        vel[me, c : c + 1, :] = jnp.sum(sums[c].T, axis=0, keepdims=True)
+
+    def send_vel(i):
+        pltpu.make_async_remote_copy(
+            src_ref=vel.at[me],
+            dst_ref=vel.at[me],
+            send_sem=vel_send.at[0],
+            recv_sem=vel_recv.at[0],
+            device_id=dev(i),
+            device_id_type=MESH,
+        ).start()
+
+    partners(1, n, send_vel)
+
     tags = gath.at[pl.ds(0, n // 16)]
     pltpu.make_async_copy(tags, tags, tag_sem.at[1]).wait()
 
@@ -419,8 +434,6 @@
 
     def put_out(c, x, value):
         out_v[c, x] = value
-
-    inside(mid_v, put_out)
 
     loads[3].wait()
     guarded(has[0], diag_copy.wait_recv)
@@ -443,17 +456,93 @@
     share_v[0 : 4 * cy] = high
     share_v[4 * cy : 8 * cy] = rest
 
-    @pl.loop(0, n_pair, unroll=2)
-    def _(q):
-        picked = jnp.dot(share_v[...], zt[:, columns(q)], preferred_element_type=jnp.float32)
-        picked = picked[: 4 * cy] + picked[4 * cy :]
-        key_own = keys[q, 0, 0:1, :]
-        key_next = keys[q, 1, 0:1, :]
-        total = jnp.where(y_id == key_own, picked[:cy], 0.0)
-        total += jnp.where(y_id - 1 == key_own, picked[cy : 2 * cy], 0.0)
-        total += jnp.where(y_id + 1 == key_own, picked[2 * cy : 3 * cy], 0.0)
-        total += jnp.where(y_id == key_next, picked[3 * cy :], 0.0)
-        heed[q] = total
+    row8 = lax.broadcasted_iota(jnp.int32, (8, LANES), 0)
+    low1 = lax.broadcasted_iota(jnp.int32, (8, LANES), 1) < cap
+
+    def diagonal(q, value):
+        value = jnp.where(row8 == q // 2, value, 0.0)
+        high = value.astype(jnp.bfloat16).astype(jnp.float32)
+        return jnp.concatenate([high, value - high], axis=0).astype(jnp.bfloat16)
+
+    def told(lhs_rows, names):
+        return lax.dot_general(
+            lhs_rows, names, (((1,), (1,)), ((), ())), preferred_element_type=jnp.float32
+        )
+
+    if compact:
+        block = 2 * LANES
+        owner_id = lax.broadcasted_iota(jnp.int32, (8, block), 0)
+        owners = []
+        for k in range(n_blk):
+            owners.append(
+                jnp.concatenate([gath[4 * k + 1, 7:8, :], gath[4 * k + 3, 7:8, :]], axis=1)
+            )
+            same = owner_id == owners[k].astype(jnp.int32)
+            mask_v[8 * k : 8 * k + 8, :] = jnp.where(same, 1.0, 0.0)
+        before = lax.broadcasted_iota(jnp.int32, (block, block), 0) < lax.broadcasted_iota(
+            jnp.int32, (block, block), 1
+        )
+        before = jnp.where(before, 1.0, 0.0).astype(jnp.bfloat16)
+        ranks = jnp.dot(
+            mask_v[...].astype(jnp.bfloat16), before, preferred_element_type=jnp.float32
+        )
+        for k in range(n_blk):
+            part = slice(8 * k, 8 * k + 8)
+            rank = jnp.sum(ranks[part] * mask_v[part, :], axis=0, keepdims=True)
+            spot_v[k : k + 1, :] = owners[k] * cap + rank
+        name_id = lax.broadcasted_iota(jnp.int32, (LANES, block), 0)
+
+        def naming(target, first):
+            for k in range(n_blk):
+                spot = jnp.broadcast_to(spot_v[k : k + 1, :].astype(jnp.int32), (LANES, block))
+                target[0:LANES, block * k : block * (k + 1)] = jnp.where(
+                    name_id + first == spot, 1.0, 0.0
+                ).astype(jnp.bfloat16)
+
+        naming(near_v, b * cap)
+        for q in range(n_pair):
+            picked = jnp.dot(share_v[...], zt[:, columns(q)], preferred_element_type=jnp.float32)
+            picked = picked[: 4 * cy] + picked[4 * cy :]
+            key_own = keys[q, 0, 0:1, :]
+            key_next = keys[q, 1, 0:1, :]
+            mine = jnp.where(y_id == key_own, picked[:cy], 0.0)
+            mine += jnp.where(y_id == key_next, picked[3 * cy :], 0.0)
+            below = jnp.where(y_id - 1 == key_own, picked[cy : 2 * cy], 0.0)
+            above = jnp.where(y_id + 1 == key_own, picked[2 * cy : 3 * cy], 0.0)
+            for k, value in enumerate((mine, below, above)):
+                coef_v[16 * k : 16 * k + 16, columns(q)] = diagonal(
+                    q, jnp.sum(value, axis=0, keepdims=True)
+                )
+        picked = told(coef_v[...], near_v[...])
+        picked = [picked[16 * k : 16 * k + 8] + picked[16 * k + 8 : 16 * k + 16] for k in range(3)]
+        msg[b, 0] = picked[0]
+        msg[b, 1] = jnp.where(low1, picked[1], pltpu.roll(picked[2], cap, 1))
+
+        def send_msg(i):
+            pltpu.make_async_remote_copy(
+                src_ref=msg.at[b],
+                dst_ref=msg.at[b],
+                send_sem=msg_sem.at[0],
+                recv_sem=msg_sem.at[1],
+                device_id=(blk_to(i), j),
+                device_id_type=MESH,
+            ).start()
+
+        partners(1, n_blk, send_msg)
+    else:
+        @pl.loop(0, n_pair, unroll=2)
+        def _(q):
+            picked = jnp.dot(share_v[...], zt[:, columns(q)], preferred_element_type=jnp.float32)
+            picked = picked[: 4 * cy] + picked[4 * cy :]
+            key_own = keys[q, 0, 0:1, :]
+            key_next = keys[q, 1, 0:1, :]
+            total = jnp.where(y_id == key_own, picked[:cy], 0.0)
+            total += jnp.where(y_id - 1 == key_own, picked[cy : 2 * cy], 0.0)
+            total += jnp.where(y_id + 1 == key_own, picked[2 * cy : 3 * cy], 0.0)
+            total += jnp.where(y_id == key_next, picked[3 * cy :], 0.0)
+            heed[q] = total
+
+    inside(mid_v, put_out)
 
     for k in range(4):
         guarded(arrives[k], halo1[k].wait_recv)
@@ -463,20 +552,6 @@
     for x in range(1, cx):
         profile += circ_v[x] * out_v[1, x]
     profile = sum(profile[:, k : k + LANES] for k in range(0, cz, LANES))
-
-    others = vel.at[pl.ds(0, n - 1)]
-    pltpu.make_async_copy(others, others, vel_recv.at[0]).wait()
-
-    def heeded(q, total):
-        return total + heed[q] * (vel[2 * q, 1:2, :] + vel[2 * q + 1, 1:2, :])
-
-    if n_pair <= 32:
-        for q in range(n_pair):
-            profile = heeded(q, profile)
-    else:
-        profile = lax.fori_loop(0, n_pair, heeded, profile)
-    folded = jnp.concatenate([profile, jnp.zeros((LANES - cy, LANES), jnp.float32)], axis=0)
-    prof[b] = jnp.sum(folded.T, axis=0, keepdims=True)
 
     def send_prof(i):
         pltpu.make_async_remote_copy(
@@ -488,7 +563,38 @@
             device_id_type=MESH,
         ).start()
 
-    partners(1, n_blk, send_prof)
+    def give_profile(profile):
+        folded = jnp.concatenate([profile, jnp.zeros((LANES - cy, LANES), jnp.float32)], axis=0)
+        prof[b] = jnp.sum(folded.T, axis=0, keepdims=True)
+        partners(1, n_blk, send_prof)
+
+    if compact:
+        give_profile(profile)
+        for k in range(n_blk * cap // LANES):
+            naming(name_v.at[pl.ds(k * LANES, LANES)], k * LANES)
+        for q in range(n_pair):
+            row = (gath[2 * q, 7:8, :].astype(jnp.int32) >> zbits) - j * cy
+            line_v[:, columns(q)] = diagonal(q, row.astype(jnp.float32))
+        rows_at = told(line_v[...], name_v[...])[:8]
+
+    others = vel.at[pl.ds(0, n - 1)]
+    pltpu.make_async_copy(others, others, vel_recv.at[0]).wait()
+
+    if compact:
+        for q in range(n_pair):
+            line_v[:, columns(q)] = diagonal(q, vel[2 * q, 1:2, :] + vel[2 * q + 1, 1:2, :])
+        moved = told(line_v[...], name_v[...])
+        moved = moved[:8] + moved[8:]
+    else:
+        def heeded(q, total):
+            return total + heed[q] * (vel[2 * q, 1:2, :] + vel[2 * q + 1, 1:2, :])
+
+        if n_pair <= 32:
+            for q in range(n_pair):
+                profile = heeded(q, profile)
+        else:
+            profile = lax.fori_loop(0, n_pair, heeded, profile)
+        give_profile(profile)
 
     edge_id = jnp.where(y_id >= 6, -2, jnp.where((y_id & 1) == 0, -1, cy))
     n_row = 7 * cy
@@ -540,9 +646,36 @@
 
     table = prof[:, 0, :].T
     place_id = place_v[0:1].astype(jnp.int32)
+    if compact:
+        messages = msg.at[pl.ds(0, n_blk - 1)]
+        pltpu.make_async_copy(messages, messages, msg_sem.at[0]).wait()
+        pltpu.make_async_copy(messages, messages, msg_sem.at[1]).wait()
+
+        def lists(value, o):
+            i = o // 2
+            pair_of = value[:, i * LANES : (i + 1) * LANES]
+            turned = pltpu.roll(pair_of, cap, 1)
+            if o % 2 == 0:
+                return pair_of, jnp.where(low1, pair_of, turned)
+            i = min(i + 1, n_blk // 2 - 1)
+            after = pltpu.roll(value[:, i * LANES : (i + 1) * LANES], cap, 1)
+            return jnp.where(low1, turned, after), jnp.where(low1, turned, pair_of)
+
+        beside_row = jnp.where(low1, 1.0, -1.0)
     looked = jnp.zeros((cy, LANES), jnp.float32)
     for k in range(n_blk):
-        looked += jnp.where(y_id + k * cy == place_id, table[:cy, k : k + 1], 0.0)
+        column = table[:cy, k : k + 1]
+        if compact:
+            gain = jnp.zeros((cy, LANES), jnp.float32)
+            value, double = lists(moved, k)
+            at, at_own = lists(rows_at, k)
+            for f, (x, y) in enumerate(((value, at), (double, at_own + beside_row))):
+                x = x * msg[k, f]
+                y = y.astype(jnp.int32)
+                for r in range(8):
+                    gain += jnp.where(y_id == y[r : r + 1], x[r : r + 1], 0.0)
+            column = column + jnp.sum(gain, axis=1, keepdims=True)
+        looked += jnp.where(y_id + k * cy == place_id, column, 0.0)
     looked = jnp.sum(looked, axis=0, keepdims=True)
     ng_ref[...] = (1.0 - RELAX) * gam_ref[...] + RELAX * looked
 
@@ -621,7 +754,15 @@
             pltpu.VMEM((8 * cy, cz), jnp.bfloat16),
             pltpu.VMEM((n // 2, cy, LANES), f32),
             pltpu.VMEM((3, LANES, LANES), f32),
+            pltpu.VMEM((64, 2 * LANES), f32),
+            pltpu.VMEM((8, 2 * LANES), f32),
+            pltpu.VMEM((LANES, 16 * LANES), jnp.bfloat16),
+            pltpu.VMEM((48, 16 * LANES), jnp.bfloat16),
+            pltpu.VMEM((4 * LANES, 16 * LANES), jnp.bfloat16),
+            pltpu.VMEM((16, 16 * LANES), jnp.bfloat16),
+            pltpu.VMEM((8, 2, 8, LANES), f32),
             dma((10,)),
+            dma((2,)),
             dma((2,)),
             dma((1,)),
             dma((n // 4,)),

time: 22.4 us -> 21.9 us (0.978)
  Pallas kernels: 21.6 us -> 21.1 us
    pallas_call x1, Pallas kernels: 20.8 us -> 20.3 us  [per_device(): pl.pallas_call(functools.partial(kernel, n_blk, n_bld), out_shape=(pltpu....]
where the time goes in v5:
time: 21.9 us; the launch traced here: 21.8 us
  Pallas kernels  21.1 us (96%)
  between operations  0.64 us (3%)
    pallas_call x1, Pallas kernels, per_device(): pl.pallas_call(functools.partial(kernel, n_blk, n_bld), out_shape=(pltpu....  20.3 us
    pallas_call x1, Pallas kernels, per_device(): pl.pallas_call(hand_over, out_shape=(jax.ShapeDtypeStruct(flow.shape, f32...  0.78 us

profile of v5, /device:TPU:0, one launch (start us, length us, event | category | flops | bytes accessed | tf_op | source)
XLA Modules:
  0.0 21.8 jit_solution(10451628840182457459)
XLA Ops:
  0.6 20.3 %shard_map.140 = (f32[3,8,16,256]{3,2,1,0:T(8,128)S(1)}, f32[1,128]{1,0:T(1,128)S(1)}) custom-call(f32[3,256]{1,0:T(4,128)} %pos_hbm.1, s32[2,128]{1,0:T(2,128)} %bitcast.2, s32[2,128]{1,0:T(2,128)} %bitcast.3, f32[3,1,128]{2,1,0:T(1,128)} %start_hbm.1, f32[3,1,128]{2,1,0:T(1,128)} %step_hbm.1, f32[1,128]{1,0:T(1,128)} %gam_hbm.1, s32[1,128]{1,0:T(1,128)} %sec_hbm.1, ...), custom_call_target="tpu_custom_call" | custom-call | tf_op jit(solution)/shard_map/pallas_call | solution.py:720
  21.0 0.8 %shard_map.141 = (f32[3,8,16,256]{3,2,1,0:T(8,128)}, f32[1,128]{1,0:T(1,128)}) custom-call(f32[3,8,16,256]{3,2,1,0:T(8,128)S(1)} %get-tuple-element.4.flow_v, f32[1,128]{1,0:T(1,128)S(1)} %get-tuple-element.5.gamma_v), custom_call_target="tpu_custom_call" | custom-call | tf_op jit(solution)/shard_map/pallas_call | solution.py:794

commit v6 on v5

--- a/solution.py
+++ b/solution.py
@@ -13,7 +13,7 @@
 OMEGA = 0.8
 RELAX = 0.5
 LANES = 128
-EARLY = 6
+EARLY = 0
 MESH = pl.DeviceIdType.MESH
 
 
@@ -197,35 +197,71 @@
             device_id_type=MESH,
         ).start()
 
-    partners(1, n // 2, send_wake)
-    partners(0, n // 2, send_tag)
-
     has = (b < n_blk - 1, b > 0, j < n_bld - 1, j > 0)
     nxt_b, prv_b = (b + 1, j), (b - 1, j)
     nxt_j, prv_j = (b, j + 1), (b, j - 1)
 
+    slot_of = {1: 0, 0: 2, 2: 3}
+
     def halo_copies(stage):
-        base = 4 * stage
-        to_next = flow_ref.at[:, cx - 1] if stage == 0 else mid_v.at[:, cx]
-        to_prev = flow_ref.at[:, 0] if stage == 0 else mid_v.at[:, 1]
         grid = flow_v if stage == 0 else mid_v
-        pairs = [
-            (to_next, grid.at[:, 0], nxt_b, 0),
-            (to_prev, grid.at[:, cx + 1], prv_b, 1),
-            (ysend.at[stage, 0], yrecv.at[stage, 0], nxt_j, 2),
-            (ysend.at[stage, 1], yrecv.at[stage, 1], prv_j, 3),
-        ]
-        return [
-            pltpu.make_async_remote_copy(
-                src_ref=s,
-                dst_ref=d,
-                send_sem=halo_send.at[base + k],
-                recv_sem=halo_recv.at[base + k],
-                device_id=to,
-                device_id_type=MESH,
+
+        def edge(c, x):
+            return flow_ref.at[c, x] if stage == 0 else mid_v.at[c, x + 1]
+
+        rows = (pl.ds(0, 2 if stage == 0 else 1), pl.ds(2, 2))
+        out = []
+        for group in range(2):
+            pieces = [[], [], [], []]
+            for c in ((1,), (0, 2))[group]:
+                pieces[0].append((edge(c, cx - 1), grid.at[c, 0], nxt_b))
+                pieces[1].append((edge(c, 0), grid.at[c, cx + 1], prv_b))
+            for k, to in ((2, nxt_j), (3, prv_j)):
+                part = rows[group]
+                pieces[k].append((ysend.at[stage, k - 2, part], yrecv.at[stage, k - 2, part], to))
+            out.append(
+                [
+                    [
+                        pltpu.make_async_remote_copy(
+                            src_ref=s,
+                            dst_ref=d,
+                            send_sem=halo_send.at[4 * stage + k],
+                            recv_sem=halo_recv.at[8 * stage + 4 * group + k],
+                            device_id=to,
+                            device_id_type=MESH,
+                        )
+                        for s, d, to in pieces[k]
+                    ]
+                    for k in range(4)
+                ]
             )
-            for s, d, to, k in pairs
-        ]
+        return out
+
+    def halo_start(stage, group, k):
+        def start():
+            for copy in halos[stage][group][k]:
+                copy.start()
+
+        guarded(has[k], start)
+
+    def halo_landed(stage, group):
+        for k in range(4):
+            if group == 1 and k < 2:
+                both = flow_v.at[pl.ds(0, 2), 0]
+                landed_copy = pltpu.make_async_copy(
+                    both, both, halo_recv.at[8 * stage + 4 + k]
+                )
+                guarded(arrives[k], landed_copy.wait)
+            else:
+                guarded(arrives[k], halos[stage][group][k][0].wait_recv)
+
+    def halo_sent(stage):
+        for k in range(4):
+            if k < 2:
+                gone = flow_v.at[:, 0]
+            else:
+                gone = ysend.at[stage, 0, pl.ds(0, 4 if stage == 0 else 3)]
+            guarded(has[k], pltpu.make_async_copy(gone, gone, halo_send.at[4 * stage + k]).wait)
 
     def guarded(cond, action):
         @pl.when(cond)
@@ -236,27 +272,31 @@
         src_ref=diag_ref.at[0],
         dst_ref=dgn_v,
         send_sem=halo_send.at[8],
-        recv_sem=halo_recv.at[8],
+        recv_sem=halo_recv.at[16],
         device_id=prv_b,
         device_id_type=MESH,
     )
-    halo0 = halo_copies(0)
-    halo1 = halo_copies(1)
-    guarded(has[0], halo0[0].start)
-    guarded(has[1], halo0[1].start)
+    halos = (halo_copies(0), halo_copies(1))
 
     arrives = (has[1], has[0], has[3], has[2])
+
+    halo_start(0, 0, 0)
+    halo_start(0, 0, 1)
+    partners(1, n // 2, send_wake)
 
     loads[0].wait()
     loads[1].wait()
     for c in range(3):
-        ysend[0, 0, c] = flow_v[c, 1 : cx + 1, cy - 1, :]
-        ysend[0, 1, c] = flow_v[c, 1 : cx + 1, 0, :]
-    ysend[0, 0, 3] = diag_v[:, cy - 1, :]
-    ysend[0, 1, 3] = diag_v[:, 0, :]
-    guarded(has[2], halo0[2].start)
-    guarded(has[3], halo0[3].start)
+        ysend[0, 0, slot_of[c]] = flow_v[c, 1 : cx + 1, cy - 1, :]
+        ysend[0, 1, slot_of[c]] = flow_v[c, 1 : cx + 1, 0, :]
+    ysend[0, 0, 1] = diag_v[:, cy - 1, :]
+    ysend[0, 1, 1] = diag_v[:, 0, :]
+    halo_start(0, 0, 2)
+    halo_start(0, 0, 3)
+    partners(0, n // 2, send_tag)
     guarded(has[1], diag_copy.start)
+    for k in range(4):
+        halo_start(0, 1, k)
 
     @pl.when(b == 0)
     def _():
@@ -309,10 +349,10 @@
         total += jnp.where(row_id == cy - 1, right, pltpu.roll(u, cy - 1, 0))
         return total + beside_lane(u)
 
-    def inside(grid, put):
+    def inside(grid, put, parts=(0, 1, 2)):
         def plane(x, sides):
             m = m_v[x]
-            for c in range(3):
+            for c in parts:
                 u = grid[c, x + 1]
                 beside = beside_plane(u, 0.0, 0.0)
                 for side in sides:
@@ -323,12 +363,12 @@
         pl.loop(1, cx - 1)(lambda x: plane(x, (-1, 1)))
         plane(cx - 1, (-1,))
 
-    def edges(grid, stage, out, base):
-        for c in range(3):
+    def edges(grid, stage, out, base, parts):
+        for c in parts:
             out[c, base] += m_v[0] * grid[c, 0]
             out[c, base + cx - 1] += m_v[cx - 1] * grid[c, cx + 1]
             for side, row in ((0, 0), (1, cy - 1)):
-                out[c, base : base + cx, row, :] += m_v[:, row, :] * yrecv[stage, side, c]
+                out[c, base : base + cx, row, :] += m_v[:, row, :] * yrecv[stage, side, slot_of[c]]
 
     @pl.loop(0, cx)
     def _(x):
@@ -377,26 +417,25 @@
     wake_wait(0, 1)
     wake_from(1)
 
+    def second_edges(parts, group):
+        halo_landed(0, group)
+        edges(flow_v, 0, mid_v, 1, parts)
+        for c in parts:
+            ysend[1, 0, slot_of[c]] = mid_v[c, 1 : cx + 1, cy - 1, :]
+            ysend[1, 1, slot_of[c]] = mid_v[c, 1 : cx + 1, 0, :]
+        for k in range(4):
+            halo_start(1, group, k)
+
     def wake_pair(k):
         wake_wait(k, 2)
         wake_from(2 * k)
         wake_from(2 * k + 1)
 
     early = max(1, EARLY * n // 32)
-    pl.loop(1, early)(wake_pair)
-
-    for k in range(4):
-        guarded(arrives[k], halo0[k].wait_recv)
-    edges(flow_v, 0, mid_v, 1)
-    for c in range(3):
-        ysend[1, 0, c] = mid_v[c, 1 : cx + 1, cy - 1, :]
-        ysend[1, 1, c] = mid_v[c, 1 : cx + 1, 0, :]
-    ysend[1, 0, 3] = jnp.zeros((cx, cz), jnp.float32)
-    ysend[1, 1, 3] = jnp.zeros((cx, cz), jnp.float32)
-    for k in range(4):
-        guarded(has[k], halo1[k].start)
-
-
+    if early > 1:
+        pl.loop(1, early)(wake_pair)
+
+    second_edges((1,), 0)
     pl.loop(early, n // 4)(wake_pair)
     for c in range(3):
         vel[me, c : c + 1, :] = jnp.sum(sums[c].T, axis=0, keepdims=True)
@@ -412,6 +451,7 @@
         ).start()
 
     partners(1, n, send_vel)
+    second_edges((0, 2), 1)
 
     tags = gath.at[pl.ds(0, n // 16)]
     pltpu.make_async_copy(tags, tags, tag_sem.at[1]).wait()
@@ -439,8 +479,8 @@
     guarded(has[0], diag_copy.wait_recv)
     m_first, m_second, m_last = m_v[0], m_v[1], m_v[cx - 1]
     m_next = OMEGA / (6.0 + dgn_v[...])
-    m_left = OMEGA / (6.0 + yrecv[0, 0, 3, 0:1, :])
-    m_right = OMEGA / (6.0 + yrecv[0, 1, 3, 0:1, :])
+    m_left = OMEGA / (6.0 + yrecv[0, 0, 1, 0:1, :])
+    m_right = OMEGA / (6.0 + yrecv[0, 1, 1, 0:1, :])
     reach = circ_v[0] * m_first
     share = jnp.concatenate(
         [
@@ -492,14 +532,12 @@
             spot_v[k : k + 1, :] = owners[k] * cap + rank
         name_id = lax.broadcasted_iota(jnp.int32, (LANES, block), 0)
 
-        def naming(target, first):
-            for k in range(n_blk):
-                spot = jnp.broadcast_to(spot_v[k : k + 1, :].astype(jnp.int32), (LANES, block))
-                target[0:LANES, block * k : block * (k + 1)] = jnp.where(
-                    name_id + first == spot, 1.0, 0.0
-                ).astype(jnp.bfloat16)
-
-        naming(near_v, b * cap)
+        first = b * cap
+        for k in range(n_blk):
+            spot = jnp.broadcast_to(spot_v[k : k + 1, :].astype(jnp.int32), (LANES, block))
+            near_v[:, block * k : block * (k + 1)] = jnp.where(
+                name_id + first == spot, 1.0, 0.0
+            ).astype(jnp.bfloat16)
         for q in range(n_pair):
             picked = jnp.dot(share_v[...], zt[:, columns(q)], preferred_element_type=jnp.float32)
             picked = picked[: 4 * cy] + picked[4 * cy :]
@@ -542,11 +580,9 @@
             total += jnp.where(y_id == key_next, picked[3 * cy :], 0.0)
             heed[q] = total
 
-    inside(mid_v, put_out)
-
-    for k in range(4):
-        guarded(arrives[k], halo1[k].wait_recv)
-    edges(mid_v, 1, out_v, 0)
+    inside(mid_v, put_out, (1,))
+    halo_landed(1, 0)
+    edges(mid_v, 1, out_v, 0, (1,))
 
     profile = circ_v[0] * out_v[1, 0]
     for x in range(1, cx):
@@ -570,12 +606,20 @@
 
     if compact:
         give_profile(profile)
-        for k in range(n_blk * cap // LANES):
-            naming(name_v.at[pl.ds(k * LANES, LANES)], k * LANES)
+    inside(mid_v, put_out, (0, 2))
+    if compact:
+        names = n_blk * cap
+        down = spot_v[...].T
+        across = lax.broadcasted_iota(jnp.int32, (block, names), 1)
+        for k in range(n_blk):
+            spot = jnp.broadcast_to(down[:, k : k + 1].astype(jnp.int32), (block, names))
+            name_v[block * k : block * (k + 1), :] = jnp.where(
+                across == spot, 1.0, 0.0
+            ).astype(jnp.bfloat16)
         for q in range(n_pair):
             row = (gath[2 * q, 7:8, :].astype(jnp.int32) >> zbits) - j * cy
             line_v[:, columns(q)] = diagonal(q, row.astype(jnp.float32))
-        rows_at = told(line_v[...], name_v[...])[:8]
+        rows_at = jnp.dot(line_v[...], name_v[...], preferred_element_type=jnp.float32)[:8]
 
     others = vel.at[pl.ds(0, n - 1)]
     pltpu.make_async_copy(others, others, vel_recv.at[0]).wait()
@@ -583,7 +627,7 @@
     if compact:
         for q in range(n_pair):
             line_v[:, columns(q)] = diagonal(q, vel[2 * q, 1:2, :] + vel[2 * q + 1, 1:2, :])
-        moved = told(line_v[...], name_v[...])
+        moved = jnp.dot(line_v[...], name_v[...], preferred_element_type=jnp.float32)
         moved = moved[:8] + moved[8:]
     else:
         def heeded(q, total):
@@ -596,26 +640,30 @@
             profile = lax.fori_loop(0, n_pair, heeded, profile)
         give_profile(profile)
 
+    halo_landed(1, 1)
+    edges(mid_v, 1, out_v, 0, (0, 2))
+
     edge_id = jnp.where(y_id >= 6, -2, jnp.where((y_id & 1) == 0, -1, cy))
     n_row = 7 * cy
 
-    @pl.loop(0, n_pair, unroll=4)
+    @pl.loop(0, n_pair, unroll=min(n_pair, 16))
     def _(q):
         v = tuple(vel[2 * q, c : c + 1, :] + vel[2 * q + 1, c : c + 1, :] for c in range(3))
+        high = tuple(x.astype(jnp.bfloat16).astype(jnp.float32) for x in v)
+        split = (high, tuple(x - y for x, y in zip(v, high)))
         key_own = keys[q, 0, 0:1, :]
         key_next = keys[q, 1, 0:1, :]
         own = y_id == key_own
         nxt = y_id == key_next
         edge = edge_id == key_own
-        v_edge = jnp.where(y_id < 2, v[0], jnp.where(y_id < 4, v[1], v[2]))
-        parts = [jnp.where(own, v[c], 0.0) for c in range(3)]
-        parts += [jnp.where(nxt, v[c], 0.0) for c in range(3)]
-        parts += [jnp.where(edge, v_edge, 0.0)]
-        for k, part in enumerate(parts):
-            high = part.astype(jnp.bfloat16)
-            rest = (part - high.astype(jnp.float32)).astype(jnp.bfloat16)
-            lhs[k * cy : (k + 1) * cy, columns(q)] = high
-            lhs[n_row + k * cy : n_row + (k + 1) * cy, columns(q)] = rest
+        for half, w in enumerate(split):
+            w_edge = jnp.where(y_id < 2, w[0], jnp.where(y_id < 4, w[1], w[2]))
+            parts = [jnp.where(own, w[c], 0.0) for c in range(3)]
+            parts += [jnp.where(nxt, w[c], 0.0) for c in range(3)]
+            parts += [jnp.where(edge, w_edge, 0.0)]
+            for k, part in enumerate(parts):
+                first = half * n_row + k * cy
+                lhs[first : first + cy, columns(q)] = part.astype(jnp.bfloat16)
 
     dot = lax.dot_general(
         lhs[...], zt[...], (((1,), (1,)), ((), ())), preferred_element_type=jnp.float32
@@ -631,24 +679,13 @@
         out_v[c, 1] += m_v[1] * one
         out_v[c, cx - 1] += m_v[cx - 1] * (m_next * face[(3 + c) * cy : (4 + c) * cy])
 
-    sent = gath.at[pl.ds(0, n // 2 - 1)]
-    pltpu.make_async_copy(sent, sent, wake_send.at[0]).wait()
-    pltpu.make_async_copy(tags, tags, tag_sem.at[0]).wait()
-    pltpu.make_async_copy(others, others, vel_send.at[0]).wait()
-    for k in range(4):
-        guarded(has[k], halo0[k].wait_send)
-        guarded(has[k], halo1[k].wait_send)
-    guarded(has[1], diag_copy.wait_send)
-
     blocks = prof.at[pl.ds(0, n_blk - 1)]
-    pltpu.make_async_copy(blocks, blocks, prof_send.at[0]).wait()
     pltpu.make_async_copy(blocks, blocks, prof_recv.at[0]).wait()
 
     table = prof[:, 0, :].T
     place_id = place_v[0:1].astype(jnp.int32)
     if compact:
         messages = msg.at[pl.ds(0, n_blk - 1)]
-        pltpu.make_async_copy(messages, messages, msg_sem.at[0]).wait()
         pltpu.make_async_copy(messages, messages, msg_sem.at[1]).wait()
 
         def lists(value, o):
@@ -678,6 +715,17 @@
         looked += jnp.where(y_id + k * cy == place_id, column, 0.0)
     looked = jnp.sum(looked, axis=0, keepdims=True)
     ng_ref[...] = (1.0 - RELAX) * gam_ref[...] + RELAX * looked
+
+    sent = gath.at[pl.ds(0, n // 2 - 1)]
+    pltpu.make_async_copy(sent, sent, wake_send.at[0]).wait()
+    pltpu.make_async_copy(tags, tags, tag_sem.at[0]).wait()
+    pltpu.make_async_copy(others, others, vel_send.at[0]).wait()
+    halo_sent(0)
+    halo_sent(1)
+    guarded(has[1], diag_copy.wait_send)
+    pltpu.make_async_copy(blocks, blocks, prof_send.at[0]).wait()
+    if compact:
+        pltpu.make_async_copy(messages, messages, msg_sem.at[0]).wait()
 
 
 def hand_over(flow_v, gamma_v, flow_hbm, gamma_hbm, sem):
@@ -758,7 +806,7 @@
             pltpu.VMEM((8, 2 * LANES), f32),
             pltpu.VMEM((LANES, 16 * LANES), jnp.bfloat16),
             pltpu.VMEM((48, 16 * LANES), jnp.bfloat16),
-            pltpu.VMEM((4 * LANES, 16 * LANES), jnp.bfloat16),
+            pltpu.VMEM((16 * LANES, 4 * LANES), jnp.bfloat16),
             pltpu.VMEM((16, 16 * LANES), jnp.bfloat16),
             pltpu.VMEM((8, 2, 8, LANES), f32),
             dma((10,)),
@@ -771,7 +819,7 @@
             dma((1,)),
             dma((1,)),
             dma((9,)),
-            dma((9,)),
+            dma((17,)),
         ],
         compiler_params=pltpu.CompilerParams(
             collective_id=0, has_side_effects=True, vmem_limit_bytes=56 * 1024 * 1024

time: 21.9 us -> 21.4 us (0.977)
  Pallas kernels: 21.1 us -> 20.6 us
    pallas_call x1, Pallas kernels: 20.3 us -> 19.8 us  [per_device(): pl.pallas_call(functools.partial(kernel, n_blk, n_bld), out_shape=(pltpu....]
where the time goes in v6:
time: 21.4 us; the launch traced here: 21.3 us
  Pallas kernels  20.6 us (96%)
  between operations  0.64 us (3%)
    pallas_call x1, Pallas kernels, per_device(): pl.pallas_call(functools.partial(kernel, n_blk, n_bld), out_shape=(pltpu....  19.8 us
    pallas_call x1, Pallas kernels, per_device(): pl.pallas_call(hand_over, out_shape=(jax.ShapeDtypeStruct(flow.shape, f32...  0.78 us

profile of v6, /device:TPU:0, one launch (start us, length us, event | category | flops | bytes accessed | tf_op | source)
XLA Modules:
  0.0 21.3 jit_solution(14493208597954744340)
XLA Ops:
  0.6 19.8 %shard_map.140 = (f32[3,8,16,256]{3,2,1,0:T(8,128)S(1)}, f32[1,128]{1,0:T(1,128)S(1)}) custom-call(f32[3,256]{1,0:T(4,128)} %pos_hbm.1, s32[2,128]{1,0:T(2,128)} %bitcast.2, s32[2,128]{1,0:T(2,128)} %bitcast.3, f32[3,1,128]{2,1,0:T(1,128)} %start_hbm.1, f32[3,1,128]{2,1,0:T(1,128)} %step_hbm.1, f32[1,128]{1,0:T(1,128)} %gam_hbm.1, s32[1,128]{1,0:T(1,128)} %sec_hbm.1, ...), custom_call_target="tpu_custom_call" | custom-call | tf_op jit(solution)/shard_map/pallas_call | solution.py:768
  20.5 0.8 %shard_map.141 = (f32[3,8,16,256]{3,2,1,0:T(8,128)}, f32[1,128]{1,0:T(1,128)}) custom-call(f32[3,8,16,256]{3,2,1,0:T(8,128)S(1)} %get-tuple-element.4.flow_v, f32[1,128]{1,0:T(1,128)S(1)} %get-tuple-element.5.gamma_v), custom_call_target="tpu_custom_call" | custom-call | tf_op jit(solution)/shard_map/pallas_call | solution.py:842
